TPU v7x, 256 devices: a whole 4x4x8 slice. The times are simulated.
256 devices in a mesh: row: 8 (over y, core), col: 32 (over z, x).
Axes of the slice: x: 4, y: 4, z: 8, core: 2. Of those that a mesh axis runs over, the one named last changes fastest.
Arguments:
- student_image: bfloat16 [16384, 512], P(('row', 'col')), may hold values from -0.16 to 0.16
- student_text: bfloat16 [16384, 512], P(('row', 'col')), may hold values from -0.16 to 0.16
- teacher_image: bfloat16 [16384, 1280], P(('row', 'col')), may hold values from -32 to 32
- teacher_text: bfloat16 [16384, 1280], P(('row', 'col')), may hold values from -32 to 32
- teacher_scale: float32 [], replicated, may hold values from 20 to 250
- student_scale: float32 [], replicated, may hold values from 10 to 250
Outputs:
- image_grad: float32 [16384, 512], P(('row', 'col'))
- text_grad: float32 [16384, 512], P(('row', 'col'))
All inputs are finite; a program needn't handle non-finite values.
Results may differ from a plain program's by a relative error of at most 0.012.
The roundings to bfloat16 on the way count: a program that leaves them out, or rounds other values in their place, can miss the bound.
Values may be sent and summed in bfloat16 or wider, within the bound.
A program may use at most 64 MiB of HBM per device.

v0:
```python
import jax
import jax.numpy as jnp
from jax import lax
from jax.sharding import PartitionSpec as P

EPSILON = 1e-12


def unit_rows(raw):
    values = raw.astype(jnp.float32)
    inverse = lax.rsqrt(jnp.sum(values * values, axis=-1, keepdims=True) + EPSILON)
    return (values * inverse, inverse)


def scaled_logits(left, right, scale):
    product = lax.dot_general(
        left, right, (((1,), (1,)), ((), ())), preferred_element_type=jnp.float32
    )
    return scale * product


def block_stats(logits, axis):
    peak = jnp.max(logits, axis=axis)
    total = jnp.sum(jnp.exp(logits - jnp.expand_dims(peak, axis)), axis=axis)
    return (peak, total)


def join_pair(peak_a, total_a, peak_b, total_b):
    top = jnp.maximum(peak_a, peak_b)
    return (top, total_a * jnp.exp(peak_a - top) + total_b * jnp.exp(peak_b - top))


def join_stats(first, second):
    teach_peak, teach_total = join_pair(first[0], first[1], second[0], second[1])
    learn_peak, learn_total = join_pair(first[2], first[3], second[2], second[3])
    return (teach_peak, teach_total, learn_peak, learn_total)


def back_norm(grad, unit, inverse):
    return inverse * (grad - unit * jnp.sum(unit * grad, axis=-1, keepdims=True))


def body(student_image, student_text, teacher_image, teacher_text, teacher_scale, student_scale):
    image_unit, image_inverse = unit_rows(student_image)
    text_unit, text_inverse = unit_rows(student_text)
    pupil_image = image_unit.astype(jnp.bfloat16)
    pupil_text = text_unit.astype(jnp.bfloat16)
    master_image = unit_rows(teacher_image)[0].astype(jnp.bfloat16)
    master_text = unit_rows(teacher_text)[0].astype(jnp.bfloat16)
    tile_images, tile_masters = (
        lax.all_gather(pupil_image, "col", axis=0, tiled=True),
        lax.all_gather(master_image, "col", axis=0, tiled=True),
    )
    tile_texts, tile_master_texts = (
        lax.all_gather(pupil_text, "row", axis=0, tiled=True),
        lax.all_gather(master_text, "row", axis=0, tiled=True),
    )
    rows_total = tile_images.shape[0]
    columns = tile_texts.shape[0]
    width = tile_texts.shape[1]
    rows_block = min(512, rows_total)
    blocks = rows_total // rows_block
    master_blocks = tile_masters.reshape(blocks, rows_block, tile_masters.shape[1])
    pupil_blocks = tile_images.reshape(blocks, rows_block, width)

    def first_pass(carried, pieces):
        master_piece, pupil_piece = pieces
        teach = scaled_logits(master_piece, tile_master_texts, teacher_scale)
        learn = scaled_logits(pupil_piece, tile_texts, student_scale)
        teach_peak, teach_total = block_stats(teach, 0)
        learn_peak, learn_total = block_stats(learn, 0)
        updated = join_stats(carried, (teach_peak, teach_total, learn_peak, learn_total))
        return (updated, block_stats(teach, 1) + block_stats(learn, 1))

    lowest = jnp.full((columns,), -jnp.inf, jnp.float32)
    nothing = jnp.zeros((columns,), jnp.float32)
    column_local, row_blocks = lax.scan(
        first_pass, (lowest, nothing, lowest, nothing), (master_blocks, pupil_blocks)
    )
    row_local = tuple((item.reshape(rows_total) for item in row_blocks))
    row_peaks = lax.pmax((row_local[0], row_local[2]), "col")
    row_totals = lax.psum(
        (
            row_local[1] * jnp.exp(row_local[0] - row_peaks[0]),
            row_local[3] * jnp.exp(row_local[2] - row_peaks[1]),
        ),
        "col",
    )
    row_stats = (row_peaks[0], row_totals[0], row_peaks[1], row_totals[1])
    col_peaks = lax.pmax((column_local[0], column_local[2]), "row")
    col_totals = lax.psum(
        (
            column_local[1] * jnp.exp(column_local[0] - col_peaks[0]),
            column_local[3] * jnp.exp(column_local[2] - col_peaks[1]),
        ),
        "row",
    )
    column_stats = (col_peaks[0], col_totals[0], col_peaks[1], col_totals[1])
    row_split = tuple((item.reshape(blocks, rows_block) for item in row_stats))

    def second_pass(carried, pieces):
        master_piece, pupil_piece, teach_peak, teach_total, learn_peak, learn_total = pieces
        teach = scaled_logits(master_piece, tile_master_texts, teacher_scale)
        learn = scaled_logits(pupil_piece, tile_texts, student_scale)
        rows_part = (
            jnp.exp(learn - learn_peak[:, None]) / learn_total[:, None]
            - jnp.exp(teach - teach_peak[:, None]) / teach_total[:, None]
        )
        cols_part = (
            jnp.exp(learn - column_stats[2][None, :]) / column_stats[3][None, :]
            - jnp.exp(teach - column_stats[0][None, :]) / column_stats[1][None, :]
        )
        weight = (0.5 * (rows_part + cols_part)).astype(jnp.bfloat16)
        image_part = student_scale * jnp.dot(weight, tile_texts, preferred_element_type=jnp.float32)
        text_part = student_scale * lax.dot_general(
            weight, pupil_piece, (((0,), (0,)), ((), ())), preferred_element_type=jnp.float32
        )
        return (carried + text_part, image_part)

    text_partial, image_pieces = lax.scan(
        second_pass,
        jnp.zeros((columns, width), jnp.float32),
        (master_blocks, pupil_blocks) + row_split,
    )
    image_partial = image_pieces.reshape(rows_total, width)
    own_rows = student_image.shape[0]
    image_whole = lax.psum(image_partial, "col")
    text_whole = lax.psum(text_partial, "row")
    image_unit_grad = lax.dynamic_slice_in_dim(
        image_whole, lax.axis_index("col") * own_rows, own_rows, 0
    )
    text_unit_grad = lax.dynamic_slice_in_dim(
        text_whole, lax.axis_index("row") * own_rows, own_rows, 0
    )
    return (
        back_norm(image_unit_grad, image_unit, image_inverse),
        back_norm(text_unit_grad, text_unit, text_inverse),
    )


def solution(mesh):
    placed = (
        P(("row", "col"), None),
        P(("row", "col"), None),
        P(("row", "col"), None),
        P(("row", "col"), None),
        P(),
        P(),
    )
    return jax.shard_map(
        body,
        mesh=mesh,
        in_specs=placed,
        out_specs=(P(("row", "col"), None), P(("row", "col"), None)),
        check_vma=False,
    )
```

profile of v0, /device:TPU:1, one launch (start us, length us, event | category | flops | bytes accessed | tf_op | source)
XLA Modules:
  0.0 813.4 jit_solution(8702643425561794126)
XLA Ops:
  7.2 1.0 fusion.22
  8.3 1.7 fusion.23
  10.0 1.0 fusion.33
  11.0 1.6 fusion.29
  12.6 1.0 fusion.20
  13.7 1.7 fusion.21
  15.6 1.0 fusion.37
  17.5 16.6 %all_gather.13 = bf16[512,512]{1,0:T(8,128)(2,1)S(1)} all-gather(bf16[64,512]{1,0:T(8,128)(2,1)S(1)} %fusion.26), channel_id=1, replica_groups=mesh['row'=8,'col'=32] {'row'}, dimensions={0}, use_global_device_ids=true | all-gather | bytes 589824 | tf_op jit(solution)/shard_map/all_gather | solution.py:55
  34.0 6.7 all-gather.8.cloned.1.call-done
  40.8 77.5 %all-gather.4.cloned.1.call-done = bf16[2048,512]{1,0:T(8,128)(2,1)} async-done(((bf16[64,512]{1,0:T(8,128)(2,1)}), bf16[2048,512]{1,0:T(8,128)(2,1)}) %all-gather.4.cloned.1.call-update) | async-done | bytes 2097168 | tf_op jit(solution)/shard_map/all_gather | solution.py:51
  118.2 86.4 %all-gather.6.cloned.1.call-done = bf16[2048,1280]{1,0:T(8,128)(2,1)} async-done(((bf16[64,1280]{1,0:T(8,128)(2,1)}), bf16[2048,1280]{1,0:T(8,128)(2,1)}) %all-gather.6.cloned.1.call-update) | async-done | bytes 5242896 | tf_op jit(solution)/shard_map/all_gather | solution.py:52
  204.7 26.3 %while.38 = (s32[]{:T(128)}, f32[512]{0:T(512)S(1)}, f32[512]{0:T(512)S(1)}, f32[512]{0:T(512)S(1)}, f32[512]{0:T(512)S(1)}, /*index=5*/f32[4,512]{1,0:T(4,128)S...) while((s32[]{:T(128)}, f32[512]{0:T(512)S(1)}, ...), condition=%wide.region_13.14_spmd.clone, body=%wide.region_4.13_spmd.clone.sunk | while | flops 943198208 | bytes 7932087 | solution.py:77
  204.7 3.3 fusion.65
  208.4 2.2 fusion.64
  211.3 3.3 fusion.65
  215.0 2.2 fusion.64
  217.9 3.3 fusion.65
  221.6 2.2 fusion.64
  224.4 3.3 fusion.65
  228.1 2.2 fusion.64
  231.1 111.6 %all-reduce.1 = (f32[2048]{0:T(1024)S(1)}, f32[2048]{0:T(1024)S(1)}) all-reduce(f32[2048]{0:T(1024)S(1)} %bitcast.95, f32[2048]{0:T(1024)S(1)} %bitcast.97), channel_id=1, replica_groups=mesh['row'=8,'col'=32] {'col'}, use_global_device_ids=true, to_apply=%region_16.17 | all-reduce | flops 4096 | bytes 32768 | tf_op jit(solution)/shard_map/pmax | solution.py:81
  342.7 43.3 %all-reduce.3 = (f32[512]{0:T(512)S(1)}, f32[512]{0:T(512)S(1)}) all-reduce(f32[512]{0:T(512)S(1)} %get-tuple-element.178, f32[512]{0:T(512)S(1)} %get-tuple-element.180), channel_id=1, replica_groups=mesh['row'=8,'col'=32] {'row'}, use_global_device_ids=true, to_apply=%region_18.19 | all-reduce | flops 1024 | bytes 8192 | tf_op jit(solution)/shard_map/pmax | solution.py:90
  386.0 12.4 %all-reduce.2 = (f32[512]{0:T(512)S(1)}, f32[512]{0:T(512)S(1)}) all-reduce(f32[512]{0:T(512)S(1)} %get-tuple-element.379, f32[512]{0:T(512)S(1)} %get-tuple-element.378), channel_id=1, replica_groups=mesh['row'=8,'col'=32] {'row'}, use_global_device_ids=true, to_apply=%region_19.20 | all-reduce | flops 1024 | bytes 8192 | tf_op jit(solution)/shard_map/psum | solution.py:91
  398.5 109.9 %all-reduce = (f32[4,512]{1,0:T(4,128)S(1)}, f32[4,512]{1,0:T(4,128)S(1)}) all-reduce(f32[4,512]{1,0:T(4,128)S(1)} %reshape.84, f32[4,512]{1,0:T(4,128)S(1)} %reshape.88), channel_id=1, replica_groups=mesh['row'=8,'col'=32] {'col'}, use_global_device_ids=true, to_apply=%region_17.18 | all-reduce | flops 4096 | bytes 32768 | tf_op jit(solution)/shard_map/psum | solution.py:82
  508.3 41.3 %while.39 = (s32[]{:T(128)}, f32[512,512]{1,0:T(8,128)S(1)}, f32[4,512,512]{2,1,0:T(8,128)}, f32[]{:T(128)}, bf16[4,512,512]{2,1,0:T(8,128)(2,1)}, /*index=5*/bf...) while((s32[]{:T(128)}, f32[512,512]{1,0:T(8,128)S(1)}, ...), condition=%wide.region_23.24_spmd.clone, body=%wide.region_22.23_spmd.clone.sunk | while | flops 1481375744 | bytes 11571391 | solution.py:120
  508.3 3.2 convolution_multiply_fusion.7
  511.6 2.7 multiply_convert_fusion.2
  514.3 2.1 fusion.76
  516.4 2.2 fusion.75
  518.7 3.2 convolution_multiply_fusion.7
  522.0 2.7 multiply_convert_fusion.2
  524.6 2.1 fusion.76
  526.7 2.2 fusion.75
  529.0 3.2 convolution_multiply_fusion.7
  532.3 2.7 multiply_convert_fusion.2
  535.0 2.1 fusion.76
  537.0 2.2 fusion.75
  539.3 3.2 convolution_multiply_fusion.7
  542.6 2.7 multiply_convert_fusion.2
  545.2 2.2 fusion.76
  547.4 2.2 fusion.75
  549.7 1.0 copy-done
  551.3 86.7 %all-reduce.9.cloned.1.call-done = f32[512,512]{1,0:T(8,128)} async-done(((f32[512,512]{1,0:T(8,128)}), f32[512,512]{1,0:T(8,128)}) %all-reduce.9.cloned.1.call-update) | async-done | bytes 1048592 | tf_op jit(solution)/shard_map/psum | solution.py:128
  637.9 1.1 fusion.34
  639.0 1.7 fusion.36
  640.7 163.5 %all-reduce.7.cloned.1.call-done = f32[2048,512]{1,0:T(8,128)} async-done(((f32[2048,512]{1,0:T(8,128)}), f32[2048,512]{1,0:T(8,128)}) %all-reduce.7.cloned.1.call-update) | async-done | bytes 4194320 | tf_op jit(solution)/shard_map/psum | solution.py:127
  804.2 1.1 fusion.30
  805.3 1.7 fusion.32
  (76 shorter events, 5.9 us)
Async XLA Ops:
  7.2 33.6 %all-gather.8.cloned.1.call-start = ((), (), s32[]{:S(2)}) async-start(), calls=%async_computation.2 | async-start | bytes 1474560 | tf_op jit(solution)/shard_map/all_gather | solution.py:56
  10.0 108.3 %all-gather.4.cloned.1.call-start = ((), (), s32[]{:S(2)}) async-start(), calls=%async_computation | async-start | bytes 2162688 | tf_op jit(solution)/shard_map/all_gather | solution.py:51
  12.6 192.1 %all-gather.6.cloned.1.call-start = ((), (), s32[]{:S(2)}) async-start(), calls=%async_computation.1 | async-start | bytes 5406720 | tf_op jit(solution)/shard_map/all_gather | solution.py:52
  15.4 622.5 %all-reduce.9.cloned.1.call-start = ((), (), s32[]{:S(2)}) async-start(), calls=%async_computation.4 | async-start | bytes 2097152 | tf_op jit(solution)/shard_map/psum | solution.py:128
  549.7 1.0 copy-start
  550.7 253.5 %all-reduce.7.cloned.1.call-start = ((), (), s32[]{:S(2)}) async-start(), calls=%async_computation.3 | async-start | bytes 8388608 | tf_op jit(solution)/shard_map/psum | solution.py:127
  550.7 87.2 %copy-start.1 = (bf16[64,512]{1,0:T(8,128)(2,1)S(1)}, bf16[64,512]{1,0:T(8,128)(2,1)}, u32[]{:S(2)}) copy-start(bf16[64,512]{1,0:T(8,128)(2,1)} %param.11) | copy-start | bytes 196612
  550.7 253.4 %copy-start.2 = (bf16[64,512]{1,0:T(8,128)(2,1)S(1)}, bf16[64,512]{1,0:T(8,128)(2,1)}, u32[]{:S(2)}) copy-start(bf16[64,512]{1,0:T(8,128)(2,1)} %param.10) | copy-start | bytes 196612
Sparse Core Ops, SparseCore 0:
  10.1 30.6 all-gather.7
  43.9 74.2 all-gather.3
  120.8 83.8 all-gather.5
  550.8 87.0 all-reduce.8
  641.4 162.7 all-reduce.6
where the time goes:
time: 817 us; the launch traced here: 813 us
  waiting for transfers between devices  421 us (52%)
  blocking collectives  294 us (36%)
  matrix products  63.2 us (8%)
  other arithmetic  18.6 us (2%)
  between operations  14 us (2%)
    psum x1, waiting for transfers between devices, body(): image_whole = lax.psum(image_partial, 'col')  163 us
    pmax x1, blocking collectives, body(): row_peaks = lax.pmax((row_local[0], row_local[2]), 'col')  112 us
    psum x1, blocking collectives, body(): lax.psum((row_local[1] * jnp.exp(row_local[0] - row_peaks[0]), row_local[...  110 us
    psum x1, waiting for transfers between devices, body(): text_whole = lax.psum(text_partial, 'row')  86.7 us
    all_gather x1, waiting for transfers between devices, body(): lax.all_gather(master_image, 'col', axis=0, tiled=True)  86.4 us
    all_gather x1, waiting for transfers between devices, body(): lax.all_gather(pupil_image, 'col', axis=0, tiled=True)  77.5 us
    dot_general x16, matrix products, scaled_logits(): lax.dot_general(left, right, (((1,), (1,)), ((), ())), preferred_element_...  45.9 us
    pmax x1, blocking collectives, body(): col_peaks = lax.pmax((column_local[0], column_local[2]), 'row')  43.3 us
  transfers between devices with their start and end apart: 5, of which 5 were waited for; matrix products, arithmetic and copies ran while one was open for 1% of the time, Pallas kernels for 0%

commit v1 on v0

v1 whole, which is shorter than its diff:
```python
import functools
import math

import jax
import jax.numpy as jnp
from jax import lax
from jax.experimental import pallas as pl
from jax.experimental.pallas import tpu as pltpu
from jax.sharding import PartitionSpec as P

EPSILON = 1e-12
MESH = pl.DeviceIdType.MESH
NX, NY, NZ = 4, 4, 8
LOG2E = math.log2(math.e)
F32, BF16 = jnp.float32, jnp.bfloat16
COPIES = 160

PAIRS = (
    ((0, 0), (1, 0)),
    ((3, 0), (0, 1)),
    ((0, 3), (2, 0)),
    ((1, 1), (1, 3)),
    ((3, 1), (3, 3)),
    ((2, 1), (2, 3)),
    ((0, 2), (1, 2)),
    ((3, 2), (2, 2)),
)
HALF_BLOCKS = tuple(tuple((h, p, q) for h in (0, 1) for p, q in pair) for pair in PAIRS)
IMAGE_ROW = {key: g * 128 + k * 32 for g, keys in enumerate(HALF_BLOCKS) for k, key in enumerate(keys)}
TEXT_GROUPS = ((1, 7), (2, 6), (3, 5), (0, 4))
TEXT_ROW = {
    (k, sib): g * 256 + sib * 128 + i * 64
    for g, pair in enumerate(TEXT_GROUPS)
    for i, k in enumerate(pair)
    for sib in (0, 1)
}


def unit_rows(raw):
    values = raw.astype(F32)
    inverse = lax.rsqrt(jnp.sum(values * values, axis=-1, keepdims=True) + EPSILON)
    return values * inverse, inverse


def join_lse(parts):
    top = functools.reduce(jnp.maximum, parts)
    total = functools.reduce(jnp.add, [jnp.exp2(part - top) for part in parts])
    return top + jnp.log(total) * LOG2E


def back_norm(grad, raw):
    unit, inverse = unit_rows(raw)
    return inverse * (grad - unit * jnp.sum(unit * grad, axis=-1, keepdims=True))


def nt_dot(a, b):
    return lax.dot_general(a, b, (((1,), (1,)), ((), ())), preferred_element_type=F32)


def tn_dot(a, b):
    return lax.dot_general(a, b, (((0,), (0,)), ((), ())), preferred_element_type=F32)


def kernel(
    tscale_ref, sscale_ref, si_ref, st_ref, ti_ref, tt_ref, image_out, text_out,
    img, txt, teach, learn, weight, row_part, col_part, row_stat, col_stat, row_in, col_in, row_lse, col_lse,
    image_own, image_send, image_in, image_sum, image_send2, image_in2,
    text_own, text_send, text_in, text_send2, text_in2, text_half, text_in3,
    send_sem, recv_sem,
):
    ds = si_ref.shape[1]
    row, col = lax.axis_index("row"), lax.axis_index("col")
    y, core = row // 2, row % 2
    z, x = col // NX, col % NX

    def device(dx=0, dy=0, dz=0, sibling=False):
        c = 1 - core if sibling else core
        return (((y + dy) % NY) * 2 + c, ((z + dz) % NZ) * NX + (x + dx) % NX)

    def along(half, axis, d):
        return device(dx=d) if (half == 0) == (axis == 1) else device(dy=d)

    copies = []

    def send(src, dst, target):
        i = len(copies)
        copy = pltpu.make_async_remote_copy(
            src_ref=src, dst_ref=dst, send_sem=send_sem.at[i], recv_sem=recv_sem.at[i],
            device_id=target, device_id_type=MESH,
        )
        copy.start()
        copies.append(copy)
        return copy

    barrier = pltpu.get_barrier_semaphore()
    peers = [device(dx=d) for d in (1, 2, 3)] + [device(dy=d) for d in (1, 2, 3)]
    peers += [device(dz=d) for d in range(1, NZ)] + [device(sibling=True)]
    for peer in peers:
        pl.semaphore_signal(barrier, inc=1, device_id=peer, device_id_type=MESH)

    own_text = TEXT_ROW[(0, 0)]
    for start, size in ((0, 32), (32, 32)):
        for h_ref, lo, hi in ((si_ref, 0, ds), (ti_ref, ds, img.shape[1])):
            at = IMAGE_ROW[(start // 32, 0, 0)]
            img[at : at + size, lo:hi] = unit_rows(h_ref[start : start + size, :])[0].astype(BF16)
    for h_ref, lo, hi in ((st_ref, 0, ds), (tt_ref, ds, img.shape[1])):
        txt[own_text : own_text + 64, lo:hi] = unit_rows(h_ref[...])[0].astype(BF16)

    pl.semaphore_wait(barrier, len(peers))

    got = {}

    def rows(ref, at, size):
        return ref.at[pl.ds(at, size), :]

    def text_rows(k, h, sib=0):
        return rows(txt, TEXT_ROW[(k, sib)] + h * 32, 32)

    def image_rows(h, p, q, part=None):
        at = IMAGE_ROW[(h, p, q)]
        return rows(img, at, 32) if part is None else rows(img, at + part * 16, 16)

    def to_second_axis(h, p):
        got[h, p, 1] = send(image_rows(h, p, 0), image_rows(h, p, 1), along(h, 2, -1))
        got[h, p, 3] = send(image_rows(h, p, 0), image_rows(h, p, 3), along(h, 2, 1))

    def text_forward(k, h):
        if k in (0, 1, 2):
            got["t", k + 1, h] = send(text_rows(k, h), text_rows(k + 1, h), device(dz=-1))
        if k in (0, 7, 6):
            j = (k + NZ - 1) % NZ
            got["t", j, h] = send(text_rows(k, h), text_rows(j, h), device(dz=1))
        if k == 3 and h == 0:
            got["t", 4, 0] = send(text_rows(3, 0), text_rows(4, 0), device(dz=-1))
        if k == 5 and h == 1:
            got["t", 4, 1] = send(text_rows(5, 1), text_rows(4, 1), device(dz=1))
        got["s", k, h] = send(text_rows(k, h), text_rows(k, h, 1), device(sibling=True))

    def text_arrive(*ks, half):
        for k in ks:
            got["t", k, half].wait_recv()
            text_forward(k, half)

    def first_axis_arrive(p):
        for h in (0, 1):
            got[h, p, 0].wait_recv()
            part = 0 if p == 1 else 1
            d = -1 if p == 1 else 1
            got[h, 2, 0, part] = send(image_rows(h, p, 0, part), image_rows(h, 2, 0, part), along(h, 1, d))
            to_second_axis(h, p)

    def second_axis_arrive(p):
        for h in (0, 1):
            for q, part, d in ((1, 0, -1), (3, 1, 1)):
                got[h, p, q].wait_recv()
                got[h, p, 2, part] = send(image_rows(h, p, q, part), image_rows(h, p, 2, part), along(h, 2, d))

    def last_arrive(p, q):
        for h in (0, 1):
            for part in (0, 1):
                got[h, p, q, part].wait_recv()

    for h in (0, 1):
        got[h, 1, 0] = send(image_rows(h, 0, 0), image_rows(h, 1, 0), along(h, 1, -1))
        got[h, 3, 0] = send(image_rows(h, 0, 0), image_rows(h, 3, 0), along(h, 1, 1))
    for h in (0, 1):
        text_forward(0, h)
    for h in (0, 1):
        to_second_axis(h, 0)

    first_axis_arrive(1)
    first_axis_arrive(3)
    text_arrive(1, 7, half=0)
    second_axis_arrive(0)
    text_arrive(1, 7, half=1)
    last_arrive(2, 0)
    for h in (0, 1):
        to_second_axis(h, 2)
    text_arrive(2, 6, half=0)
    second_axis_arrive(1)
    text_arrive(2, 6, half=1)
    second_axis_arrive(3)
    text_arrive(3, 5, half=0)
    second_axis_arrive(2)
    last_arrive(0, 2)
    text_arrive(3, 5, half=1)
    last_arrive(1, 2)
    last_arrive(3, 2)
    text_arrive(4, half=0)
    text_arrive(4, half=1)
    last_arrive(2, 2)
    for k in range(NZ):
        for h in (0, 1):
            got["s", k, h].wait_recv()

    teach_scale = tscale_ref[0, 0] * LOG2E
    learn_scale = sscale_ref[0, 0] * LOG2E
    grad_scale = sscale_ref[0, 0]
    lane = lax.broadcasted_iota(jnp.int32, (128, 128), 1)
    line = lax.broadcasted_iota(jnp.int32, (128, 128), 0)
    spot = line % 32 + 32 * (line // 64)
    learn_spot = lane == spot
    teach_spot = lane == spot + 64

    def unit(g, tg):
        r = pl.multiple_of(g * 128, 128)
        c = pl.multiple_of(tg * 256, 256)
        lses = []
        for ref, lo, hi, scale in ((learn, 0, ds, learn_scale), (teach, ds, img.shape[1], teach_scale)):
            logits = nt_dot(img[pl.ds(r, 128), lo:hi], txt[pl.ds(c, 256), lo:hi]) * scale
            ref[pl.ds(r, 128), pl.ds(c, 256)] = logits
            top = jnp.max(logits, axis=1, keepdims=True)
            row_l = top + jnp.log(jnp.sum(jnp.exp2(logits - top), axis=1, keepdims=True)) * LOG2E
            top = jnp.max(logits, axis=0, keepdims=True)
            col_l = top + jnp.log(jnp.sum(jnp.exp2(logits - top), axis=0, keepdims=True)) * LOG2E
            lses.append((row_l, col_l))
        packed = jnp.where(learn_spot, lses[0][0], 0.0) + jnp.where(teach_spot, lses[1][0], 0.0)
        row_part[tg, g] = jnp.sum(packed.reshape(4, 32, 128), axis=1)
        col_part[g, 0:1, pl.ds(c, 256)] = lses[0][1]
        col_part[g, 1:2, pl.ds(c, 256)] = lses[1][1]

    @pl.loop(0, 4)
    def _(tg):
        @pl.loop(0, 8)
        def _(g):
            unit(g, tg)

    low = lax.broadcasted_iota(jnp.int32, (1, 128), 1) < 64
    half0 = lax.broadcasted_iota(jnp.int32, (1, 128), 1) % 64 < 32
    row_local = join_lse([row_part[tg] for tg in range(4)])

    def block_row(dy, dx):
        return ((y + dy) % NY) * NX + (x + dx) % NX

    where_is = {key: (g, k) for g, keys in enumerate(HALF_BLOCKS) for k, key in enumerate(keys)}
    for dy in range(NY):
        for dx in range(NX):
            g0, k0 = where_is[0, dx, dy]
            g1, k1 = where_is[1, dy, dx]
            line0, line1 = row_local[g0, k0 : k0 + 1, :], row_local[g1, k1 : k1 + 1, :]
            row_stat[0, pl.ds(block_row(dy, dx), 1), :] = jnp.where(half0, line0, line1)
    row_got = [send(row_stat.at[0], row_in.at[d - 1], device(dx=d)) for d in (1, 2, 3)]

    col_local = join_lse([col_part[g] for g in range(8)])

    def text_place(k, sib):
        return (1 - core if sib else core) * NZ + (z + k) % NZ

    for tg, (k0, k1) in enumerate(TEXT_GROUPS):
        for sib in (0, 1):
            c = tg * 256 + sib * 128
            ls, lt = col_local[0:1, c : c + 128], col_local[1:2, c : c + 128]
            col_stat[0, pl.ds(text_place(k0, sib), 1), :] = jnp.where(low, ls, pltpu.roll(lt, 64, 1))
            col_stat[0, pl.ds(text_place(k1, sib), 1), :] = jnp.where(low, pltpu.roll(ls, 64, 1), lt)
    col_got = send(col_stat.at[0], col_in.at[0], device(sibling=True))

    for copy in row_got:
        copy.wait_recv()
    row_stat[1] = join_lse([row_stat[0]] + [row_in[i] for i in range(3)])
    row_got = [send(row_stat.at[1], row_in.at[2 + d], device(dy=d)) for d in (1, 2, 3)]
    col_got.wait_recv()
    col_stat[1] = join_lse([col_stat[0], col_in[0]])
    col_got = [send(col_stat.at[1], col_in.at[d], device(dz=d)) for d in range(1, NZ)]
    for copy in row_got:
        copy.wait_recv()
    row_stat[2] = join_lse([row_stat[1]] + [row_in[3 + i] for i in range(3)]) + 1.0
    for dy in range(NY):
        for dx in range(NX):
            whole = row_stat[2, pl.ds(block_row(dy, dx), 1), :]
            g0, k0 = where_is[0, dx, dy]
            g1, k1 = where_is[1, dy, dx]
            row_lse[g0, k0 : k0 + 1, :] = whole
            row_lse[g1, k1 : k1 + 1, :] = whole
    for copy in col_got:
        copy.wait_recv()
    col_stat[2] = join_lse([col_stat[1]] + [col_in[d] for d in range(1, NZ)]) + 1.0
    for tg, (k0, k1) in enumerate(TEXT_GROUPS):
        for sib in (0, 1):
            c = tg * 256 + sib * 128
            line0 = col_stat[2, pl.ds(text_place(k0, sib), 1), :]
            line1 = col_stat[2, pl.ds(text_place(k1, sib), 1), :]
            col_lse[0:1, c : c + 128] = jnp.where(low, line0, pltpu.roll(line1, 64, 1))
            col_lse[1:2, c : c + 128] = jnp.where(low, pltpu.roll(line0, 64, 1), line1)

    @pl.loop(0, 8)
    def _(g):
        r = pl.multiple_of(g * 128, 128)
        lines = jnp.broadcast_to(row_lse[g][:, None, :], (4, 32, 128)).reshape(128, 128)
        learn_row = jnp.sum(jnp.where(learn_spot, lines, 0.0), axis=1, keepdims=True)
        teach_row = jnp.sum(jnp.where(teach_spot, lines, 0.0), axis=1, keepdims=True)
        for tg in range(4):
            c = slice(tg * 256, tg * 256 + 256)
            s, t = learn[pl.ds(r, 128), c], teach[pl.ds(r, 128), c]
            value = (jnp.exp2(s - learn_row) - jnp.exp2(t - teach_row)) + (
                jnp.exp2(s - col_lse[0:1, c]) - jnp.exp2(t - col_lse[1:2, c])
            )
            weight[pl.ds(r, 128), c] = value.astype(BF16)

    text_got = []
    for tg in range(4):
        c = tg * 256 + 128
        part = tn_dot(weight[:, c : c + 128], img[:, :ds]) * grad_scale
        text_send[tg] = part.astype(BF16)
        text_got.append(send(text_send.at[tg], text_in.at[tg], device(sibling=True)))
    for g, keys in enumerate(HALF_BLOCKS):
        part = jnp.dot(weight[g * 128 : g * 128 + 128, :], txt[:, :ds], preferred_element_type=F32) * grad_scale
        for k, (h, p, q) in enumerate(keys):
            piece = part[k * 32 : k * 32 + 32, :]
            if q == 0:
                image_own[h, p * 32 : p * 32 + 32, :] = piece
            else:
                image_send[h, q - 1, p * 32 : p * 32 + 32, :] = piece.astype(BF16)
    image_got = [
        [send(image_send.at[h, q - 1], image_in.at[h, q - 1], along(h, 2, q)) for q in (1, 2, 3)] for h in (0, 1)
    ]
    for tg in range(4):
        c = tg * 256
        text_own[tg] = tn_dot(weight[:, c : c + 128], img[:, :ds]) * grad_scale
    for tg in range(4):
        text_got[tg].wait_recv()
        text_own[tg] = text_own[tg] + text_in[tg].astype(F32)
    text_send2[0] = text_own[0].astype(BF16)
    text_send2[1] = text_own[2].astype(BF16)
    text_half[...] = text_own[3, 64:128, :].astype(BF16)
    merge = [
        send(text_send2.at[1, pl.ds(0, 64)], text_in2.at[1, pl.ds(0, 64)], device(dz=1)),
        send(text_half.at[pl.ds(0, 32)], text_in2.at[2, pl.ds(0, 32)], device(dz=2)),
        send(text_send2.at[1, pl.ds(64, 64)], text_in2.at[1, pl.ds(64, 64)], device(dz=-1)),
        send(text_half.at[pl.ds(32, 32)], text_in2.at[2, pl.ds(32, 32)], device(dz=-2)),
    ]
    final = [
        send(text_send2.at[0, pl.ds(0, 64)], text_in2.at[0, pl.ds(0, 64)], device(dz=1)),
        send(text_send2.at[0, pl.ds(64, 64)], text_in2.at[0, pl.ds(64, 64)], device(dz=-1)),
    ]
    for h in (0, 1):
        for copy in image_got[h]:
            copy.wait_recv()
        image_sum[h] = image_own[h] + functools.reduce(jnp.add, [image_in[h, i].astype(F32) for i in range(3)])
        image_send2[h] = image_sum[h, 32:128, :].astype(BF16)
    image_got = []
    for h in (0, 1):
        for p in (1, 2, 3):
            at = pl.ds((p - 1) * 32, 32)
            image_got.append(send(image_send2.at[h, at], image_in2.at[h, at], along(h, 1, p)))
    for copy in merge:
        copy.wait_recv()
    joined = text_own[1] + text_in2[1].astype(F32)
    extra = text_in2[2, 0:64, :].astype(F32)
    text_in3[0, 0:32, :] = (joined[0:32] + extra[0:32]).astype(BF16)
    text_in3[0, 32:96, :] = joined[32:96].astype(BF16)
    text_in3[0, 96:128, :] = (joined[96:128] + extra[32:64]).astype(BF16)
    final += [
        send(text_in3.at[0, pl.ds(0, 64)], text_in3.at[1, pl.ds(0, 64)], device(dz=2)),
        send(text_in3.at[0, pl.ds(64, 64)], text_in3.at[1, pl.ds(64, 64)], device(dz=-2)),
    ]
    for copy in image_got:
        copy.wait_recv()
    for h in (0, 1):
        at = slice(h * 32, h * 32 + 32)
        total = image_sum[h, 0:32, :] + functools.reduce(
            jnp.add, [image_in2[h, i * 32 : i * 32 + 32, :].astype(F32) for i in range(3)]
        )
        image_out[at, :] = back_norm(total, si_ref[at, :])
    for copy in final:
        copy.wait_recv()
    total = text_own[3, 0:64, :]
    for ref, i in ((text_in2, 0), (text_in3, 1)):
        total = total + ref[i, 0:64, :].astype(F32) + ref[i, 64:128, :].astype(F32)
    text_out[...] = back_norm(total, st_ref[...])
    for copy in copies:
        copy.wait_send()


def body(student_image, student_text, teacher_image, teacher_text, teacher_scale, student_scale):
    own, ds = student_image.shape
    width = ds + teacher_image.shape[1]
    vmem = pl.BlockSpec(memory_space=pltpu.VMEM)
    smem = pl.BlockSpec(memory_space=pltpu.SMEM)
    out = jax.ShapeDtypeStruct((own, ds), F32)
    return pl.pallas_call(
        kernel,
        out_shape=(out, out),
        in_specs=[smem, smem, vmem, vmem, vmem, vmem],
        out_specs=(vmem, vmem),
        scratch_shapes=[
            pltpu.VMEM((1024, width), BF16),
            pltpu.VMEM((1024, width), BF16),
            pltpu.VMEM((1024, 1024), F32),
            pltpu.VMEM((1024, 1024), F32),
            pltpu.VMEM((1024, 1024), BF16),
            pltpu.VMEM((4, 8, 4, 128), F32),
            pltpu.VMEM((8, 2, 1024), F32),
            pltpu.VMEM((3, 16, 128), F32),
            pltpu.VMEM((3, 16, 128), F32),
            pltpu.VMEM((6, 16, 128), F32),
            pltpu.VMEM((8, 16, 128), F32),
            pltpu.VMEM((8, 4, 128), F32),
            pltpu.VMEM((2, 1024), F32),
            pltpu.VMEM((2, 128, ds), F32),
            pltpu.VMEM((2, 3, 128, ds), BF16),
            pltpu.VMEM((2, 3, 128, ds), BF16),
            pltpu.VMEM((2, 128, ds), F32),
            pltpu.VMEM((2, 96, ds), BF16),
            pltpu.VMEM((2, 96, ds), BF16),
            pltpu.VMEM((4, 128, ds), F32),
            pltpu.VMEM((4, 128, ds), BF16),
            pltpu.VMEM((4, 128, ds), BF16),
            pltpu.VMEM((2, 128, ds), BF16),
            pltpu.VMEM((3, 128, ds), BF16),
            pltpu.VMEM((64, ds), BF16),
            pltpu.VMEM((2, 128, ds), BF16),
            pltpu.SemaphoreType.DMA((COPIES,)),
            pltpu.SemaphoreType.DMA((COPIES,)),
        ],
        compiler_params=pltpu.CompilerParams(
            collective_id=0, has_side_effects=True, vmem_limit_bytes=48 * 1024 * 1024
        ),
    )(
        teacher_scale.reshape(1, 1), student_scale.reshape(1, 1),
        student_image, student_text, teacher_image, teacher_text,
    )


def solution(mesh):
    placed = P(("row", "col"), None)
    return jax.shard_map(
        body,
        mesh=mesh,
        in_specs=(placed, placed, placed, placed, P(), P()),
        out_specs=(placed, placed),
        check_vma=False,
    )
```

time: 817 us -> 91.2 us (0.11)
  waiting for transfers between devices: 421 us -> 0 us
  blocking collectives: 294 us -> 0 us
  Pallas kernels: 0 us -> 83.6 us
  matrix products: 63.2 us -> 0 us
  other arithmetic: 18.6 us -> 0 us
  between operations: 14 us -> 1.94 us
    psum x2 -> x0, waiting for transfers between devices: 250 us -> none  [the longest x1 163 us: body(): image_whole = lax.psum(image_partial, 'col')]
    all_gather x3 -> x0, waiting for transfers between devices: 171 us -> none  [the longest x1 86.4 us: body(): lax.all_gather(master_image, 'col', axis=0, tiled=True)]
    pmax x2 -> x0, blocking collectives: 155 us -> none  [the longest x1 112 us: body(): row_peaks = lax.pmax((row_local[0], row_local[2]), 'col')]
    psum x2 -> x0, blocking collectives: 122 us -> none  [the longest x1 110 us: body(): lax.psum((row_local[1] * jnp.exp(row_local[0] - row_peaks[0]), row_local[...]
    pallas_call x0 -> x1, Pallas kernels: none -> 83.6 us  [body(): pl.pallas_call(kernel, out_shape=(out, out), in_specs=[smem, smem, vmem,...]
    dot_general x24 -> x0, matrix products: 63.2 us -> none  [the longest x16 45.9 us: scaled_logits(): lax.dot_general(left, right, (((1,), (1,)), ((), ())), preferred_element_...]
    all_gather x1 -> x0, blocking collectives: 16.6 us -> none  [body(): lax.all_gather(pupil_text, 'row', axis=0, tiled=True)]
    reduce_sum x14 -> x0, other arithmetic: 9.24 us -> none  [the longest x4 4.01 us: unit_rows(): jnp.sum(values * values, axis=-1, keepdims=True) + EPSILON]
  transfers between devices with their start and end apart: 5 -> 0, of which waited for: 5 -> 0; matrix products, arithmetic and copies ran while one was open for 1% -> 0% of each run, Pallas kernels for 0% -> 0%
where the time goes in v1:
time: 91.2 us; the launch traced here: 90.4 us
  Pallas kernels  83.6 us (92%)
  local copies, waits for them, and re-layouts  4.81 us (5%)
  between operations  1.94 us (2%)
    pallas_call x1, Pallas kernels, body(): pl.pallas_call(kernel, out_shape=(out, out), in_specs=[smem, smem, vmem,...  83.6 us
    unnamed x10, local copies, waits for them, and re-layouts  4.81 us

profile of v1, /device:TPU:1, one launch (start us, length us, event | category | flops | bytes accessed | tf_op | source)
XLA Modules:
  0.0 90.4 jit_solution(3439029405301230849)
XLA Ops:
  1.9 0.0 copy-start
  1.9 0.9 %copy-done = bf16[64,1280]{1,0:T(8,128)(2,1)S(1)} copy-done((bf16[64,1280]{1,0:T(8,128)(2,1)S(1)}, bf16[64,1280]{1,0:T(8,128)(2,1)}, u32[]{:S(2)}) %copy-start) | copy-done | bytes 163864
  2.8 0.0 copy-start.1
  2.8 0.9 %copy-done.1 = bf16[64,1280]{1,0:T(8,128)(2,1)S(1)} copy-done((bf16[64,1280]{1,0:T(8,128)(2,1)S(1)}, bf16[64,1280]{1,0:T(8,128)(2,1)}, u32[]{:S(2)}) %copy-start.1) | copy-done | bytes 163864
  3.8 0.0 copy-start.2
  3.8 0.8 copy-done.2
  4.6 0.0 copy-start.3
  4.6 0.8 copy-done.3
  5.4 83.6 %shard_map.77 = (f32[64,512]{1,0:T(8,128)S(1)}, f32[64,512]{1,0:T(8,128)S(1)}) custom-call(f32[1,1]{1,0:T(1,128)} %bitcast.2.tscale_ref, f32[1,1]{1,0:T(1,128)} %bitcast.3.sscale_ref, bf16[64,512]{1,0:T(8,128)(2,1)S(1)} %copy-done.2, bf16[64,512]{1,0:T(8,128)(2,1)S(1)} %copy-done.3, bf16[64,1280]{1,0:T(8,128)(2,1)S(1)} %copy-done, bf16[64,1280]{1,0:T(8,128)(2,1)S(1)} %copy-done.1), custom_call_target="tpu_custom_call" | custom-call | tf_op jit(solution)/shard_map/pallas_call | solution.py:380
  89.1 0.7 copy.12
  89.7 0.7 copy.13
Async XLA Ops:
  1.9 0.9 %copy-start = (bf16[64,1280]{1,0:T(8,128)(2,1)S(1)}, bf16[64,1280]{1,0:T(8,128)(2,1)}, u32[]{:S(2)}) copy-start(bf16[64,1280]{1,0:T(8,128)(2,1)} %ti_ref.1) | copy-start | bytes 491524
  2.8 0.9 %copy-start.1 = (bf16[64,1280]{1,0:T(8,128)(2,1)S(1)}, bf16[64,1280]{1,0:T(8,128)(2,1)}, u32[]{:S(2)}) copy-start(bf16[64,1280]{1,0:T(8,128)(2,1)} %tt_ref.1) | copy-start | bytes 491524
  3.8 0.8 copy-start.2
  4.6 0.8 copy-start.3

commit v2 on v1

v2 whole, which is shorter than its diff:
```python
import functools
import math

import jax
import jax.numpy as jnp
from jax import lax
from jax.experimental import pallas as pl
from jax.experimental.pallas import tpu as pltpu
from jax.sharding import PartitionSpec as P

EPSILON = 1e-12
MESH = pl.DeviceIdType.MESH
NX, NY, NZ = 4, 4, 8
LOG2E = math.log2(math.e)
F32, BF16 = jnp.float32, jnp.bfloat16
COPIES = 160

PAIRS = (
    ((0, 0), (1, 0)),
    ((3, 0), (0, 1)),
    ((0, 3), (2, 0)),
    ((1, 1), (1, 3)),
    ((3, 1), (3, 3)),
    ((2, 1), (2, 3)),
    ((0, 2), (1, 2)),
    ((3, 2), (2, 2)),
)
HALF_BLOCKS = tuple(tuple((h, p, q) for h in (0, 1) for p, q in pair) for pair in PAIRS)
IMAGE_ROW = {key: g * 128 + k * 32 for g, keys in enumerate(HALF_BLOCKS) for k, key in enumerate(keys)}
TEXT_BLOCKS = (
    (0, 0), (0, 1), (1, 0), (7, 0), (1, 1), (7, 1),
    (2, 0), (6, 0), (2, 1), (6, 1),
    (3, 0), (5, 0), (3, 1), (5, 1),
    (4, 0), (4, 1),
)
TEXT_ROW = {key: i * 64 for i, key in enumerate(TEXT_BLOCKS)}
COLUMNS = ((0, 384), (384, 640), (640, 896), (896, 1024))


def unit_rows(raw):
    values = raw.astype(F32)
    inverse = lax.rsqrt(jnp.sum(values * values, axis=-1, keepdims=True) + EPSILON)
    return values * inverse, inverse


def join_lse(parts):
    top = functools.reduce(jnp.maximum, parts)
    total = functools.reduce(jnp.add, [jnp.exp2(part - top) for part in parts])
    return top + jnp.log(total) * LOG2E


def back_norm(grad, raw):
    unit, inverse = unit_rows(raw)
    return inverse * (grad - unit * jnp.sum(unit * grad, axis=-1, keepdims=True))


def nt_dot(a, b):
    return lax.dot_general(a, b, (((1,), (1,)), ((), ())), preferred_element_type=F32)


def tn_dot(a, b):
    return lax.dot_general(a, b, (((0,), (0,)), ((), ())), preferred_element_type=F32)


def kernel(
    tscale_ref, sscale_ref, si_hbm, st_hbm, ti_hbm, tt_hbm, image_out, text_out,
    si_ref, st_ref, ti_ref, tt_ref, img, txt, teach, learn, weight, row_part, col_part, row_stat, col_stat, row_in, col_in, row_lse, col_lse,
    image_own, image_send, image_in, image_sum, image_send2, image_in2,
    text_own, text_send, text_in, text_send2, text_in2, text_send3, text_in3,
    send_sem, recv_sem, load_sem,
):
    ds = si_ref.shape[1]
    row, col = lax.axis_index("row"), lax.axis_index("col")
    y, core = row // 2, row % 2
    z, x = col // NX, col % NX

    def device(dx=0, dy=0, dz=0, sibling=False):
        c = 1 - core if sibling else core
        return (((y + dy) % NY) * 2 + c, ((z + dz) % NZ) * NX + (x + dx) % NX)

    def along(half, axis, d):
        return device(dx=d) if (half == 0) == (axis == 1) else device(dy=d)

    copies = []

    def send(src, dst, target):
        i = len(copies)
        copy = pltpu.make_async_remote_copy(
            src_ref=src, dst_ref=dst, send_sem=send_sem.at[i], recv_sem=recv_sem.at[i],
            device_id=target, device_id_type=MESH,
        )
        copy.start()
        copies.append(copy)
        return copy

    barrier = pltpu.get_barrier_semaphore()
    peers = [device(dx=1), device(dx=-1), device(dy=1), device(dy=-1), device(dz=1), device(dz=-1)]
    peers += [device(sibling=True)]
    for peer in peers:
        pl.semaphore_signal(barrier, inc=1, device_id=peer, device_id_type=MESH)

    loads = [
        pltpu.make_async_copy(src, dst, load_sem.at[i])
        for i, (src, dst) in enumerate(((ti_hbm, ti_ref), (tt_hbm, tt_ref), (si_hbm, si_ref), (st_hbm, st_ref)))
    ]
    for load in loads:
        load.start()
    for load in loads:
        load.wait()

    own_text = TEXT_ROW[(0, 0)]
    for start, size in ((0, 32), (32, 32)):
        for h_ref, lo, hi in ((si_ref, 0, ds), (ti_ref, ds, img.shape[1])):
            at = IMAGE_ROW[(start // 32, 0, 0)]
            img[at : at + size, lo:hi] = unit_rows(h_ref[start : start + size, :])[0].astype(BF16)
    for h_ref, lo, hi in ((st_ref, 0, ds), (tt_ref, ds, img.shape[1])):
        txt[own_text : own_text + 64, lo:hi] = unit_rows(h_ref[...])[0].astype(BF16)

    pl.semaphore_wait(barrier, len(peers))

    got = {}

    def rows(ref, at, size):
        return ref.at[pl.ds(at, size), :]

    def text_rows(k, part, size=16, sib=0):
        return rows(txt, TEXT_ROW[(k, sib)] + part * size, size)

    def image_rows(h, p, q, part=None):
        at = IMAGE_ROW[(h, p, q)]
        return rows(img, at, 32) if part is None else rows(img, at + part * 16, 16)

    def to_second_axis(h, p):
        got[h, p, 1] = send(image_rows(h, p, 0), image_rows(h, p, 1), along(h, 2, -1))
        got[h, p, 3] = send(image_rows(h, p, 0), image_rows(h, p, 3), along(h, 2, 1))

    def text_send_on(k, j, part, d):
        got["t", j, part] = send(text_rows(k, part), text_rows(j, part), device(dz=d))

    def text_to_sibling(k, half):
        got["s", k, half] = send(text_rows(k, half, 32), text_rows(k, half, 32, 1), device(sibling=True))

    def text_arrive(k, step):
        for slot, part, d in ((k, step, -1), (NZ - k, 3 - step, 1)):
            got["t", slot, part].wait_recv()
            if k < 3 or step < 2:
                text_send_on(slot, slot - d if k < 3 else 4, part, d)
            if step % 2:
                text_to_sibling(slot, part // 2)

    def text_arrive_last(step):
        for part in (step, 3 - step):
            got["t", 4, part].wait_recv()
            if step % 2:
                text_to_sibling(4, part // 2)

    def sibling_arrive(*ks):
        for k in ks:
            for half in (0, 1):
                got["s", k, half].wait_recv()

    def first_axis_arrive():
        for h in (0, 1):
            for p, part, d in ((1, 0, -1), (3, 1, 1)):
                got[h, p, 0].wait_recv()
                got[h, 2, 0, part] = send(image_rows(h, p, 0, part), image_rows(h, 2, 0, part), along(h, 1, d))
        for p in (1, 3):
            for h in (0, 1):
                to_second_axis(h, p)

    def second_axis_arrive(p):
        for h in (0, 1):
            for q, part, d in ((1, 0, -1), (3, 1, 1)):
                got[h, p, q].wait_recv()
                got[h, p, 2, part] = send(image_rows(h, p, q, part), image_rows(h, p, 2, part), along(h, 2, d))

    def last_arrive(p, q):
        for h in (0, 1):
            for part in (0, 1):
                got[h, p, q, part].wait_recv()

    teach_scale = tscale_ref[0, 0] * LOG2E
    learn_scale = sscale_ref[0, 0] * LOG2E
    grad_scale = sscale_ref[0, 0]
    lane = lax.broadcasted_iota(jnp.int32, (128, 128), 1)
    line = lax.broadcasted_iota(jnp.int32, (128, 128), 0)
    spot = line % 32 + 32 * (line // 64)
    learn_spot = lane == spot
    teach_spot = lane == spot + 64

    def logits(first, last, *blocks):
        r = slice(first * 128, last * 128)
        for b in blocks:
            c = slice(*COLUMNS[b])
            for ref, lo, hi, scale in ((learn, 0, ds, learn_scale), (teach, ds, img.shape[1], teach_scale)):
                ref[r, c] = nt_dot(img[r, lo:hi], txt[c, lo:hi]) * scale

        @pl.loop(first, last)
        def _(g):
            r = pl.multiple_of(g * 128, 128)
            for b in blocks:
                c = slice(*COLUMNS[b])
                row_ls = []
                for i, ref in enumerate((learn, teach)):
                    block = ref[pl.ds(r, 128), c]
                    top = jnp.max(block, axis=1, keepdims=True)
                    total = jnp.sum(jnp.exp2(block - top), axis=1, keepdims=True)
                    row_ls.append(top + jnp.log(total) * LOG2E)
                    top = jnp.max(block, axis=0, keepdims=True)
                    total = jnp.sum(jnp.exp2(block - top), axis=0, keepdims=True)
                    col_part[g, i : i + 1, c] = top + jnp.log(total) * LOG2E
                packed = jnp.where(learn_spot, row_ls[0], 0.0) + jnp.where(teach_spot, row_ls[1], 0.0)
                row_part[b, g] = jnp.sum(packed.reshape(4, 32, 128), axis=1)

    for step in range(4):
        text_send_on(0, 1, step, -1)
        text_send_on(0, 7, 3 - step, 1)
        if step == 0:
            for h in (0, 1):
                got[h, 1, 0] = send(image_rows(h, 0, 0), image_rows(h, 1, 0), along(h, 1, -1))
                got[h, 3, 0] = send(image_rows(h, 0, 0), image_rows(h, 3, 0), along(h, 1, 1))
    for h in (0, 1):
        to_second_axis(h, 0)
    for half in (0, 1):
        text_to_sibling(0, half)

    text_arrive(1, 0)
    first_axis_arrive()
    text_arrive(1, 1)
    text_arrive(1, 2)
    text_arrive(1, 3)
    second_axis_arrive(0)
    last_arrive(2, 0)
    for h in (0, 1):
        to_second_axis(h, 2)
    text_arrive(2, 0)
    sibling_arrive(0, 1, 7)
    logits(0, 3, 0)
    text_arrive(2, 1)
    second_axis_arrive(1)
    text_arrive(2, 2)
    logits(3, 4, 0)
    text_arrive(2, 3)
    second_axis_arrive(3)
    text_arrive(3, 0)
    logits(4, 5, 0)
    sibling_arrive(2, 6)
    logits(0, 3, 1)
    text_arrive(3, 1)
    logits(3, 5, 1)
    text_arrive(3, 2)
    second_axis_arrive(2)
    text_arrive(3, 3)
    logits(5, 6, 0, 1)
    text_arrive_last(0)
    last_arrive(0, 2)
    last_arrive(1, 2)
    sibling_arrive(3, 5)
    logits(6, 7, 0, 1)
    logits(0, 4, 2)
    text_arrive_last(1)
    logits(4, 7, 2)
    last_arrive(3, 2)
    last_arrive(2, 2)
    logits(7, 8, 0, 1, 2)
    sibling_arrive(4)
    logits(0, 8, 3)

    low = lax.broadcasted_iota(jnp.int32, (1, 128), 1) < 64
    half0 = lax.broadcasted_iota(jnp.int32, (1, 128), 1) % 64 < 32
    row_local = join_lse([row_part[tg] for tg in range(4)])

    def block_row(dy, dx):
        return ((y + dy) % NY) * NX + (x + dx) % NX

    where_is = {key: (g, k) for g, keys in enumerate(HALF_BLOCKS) for k, key in enumerate(keys)}
    for dy in range(NY):
        for dx in range(NX):
            g0, k0 = where_is[0, dx, dy]
            g1, k1 = where_is[1, dy, dx]
            line0, line1 = row_local[g0, k0 : k0 + 1, :], row_local[g1, k1 : k1 + 1, :]
            row_stat[0, pl.ds(block_row(dy, dx), 1), :] = jnp.where(half0, line0, line1)
    row_got = [send(row_stat.at[0], row_in.at[d - 1], device(dx=d)) for d in (1, 2, 3)]

    col_local = join_lse([col_part[g] for g in range(8)])

    def text_place(k, sib):
        return (1 - core if sib else core) * NZ + (z + k) % NZ

    for tile in range(8):
        c = slice(tile * 128, tile * 128 + 128)
        ls, lt = col_local[0:1, c], col_local[1:2, c]
        first, second = TEXT_BLOCKS[2 * tile : 2 * tile + 2]
        col_stat[0, pl.ds(text_place(*first), 1), :] = jnp.where(low, ls, pltpu.roll(lt, 64, 1))
        col_stat[0, pl.ds(text_place(*second), 1), :] = jnp.where(low, pltpu.roll(ls, 64, 1), lt)
    col_got = send(col_stat.at[0], col_in.at[0], device(sibling=True))

    for copy in row_got:
        copy.wait_recv()
    row_stat[1] = join_lse([row_stat[0]] + [row_in[i] for i in range(3)])
    row_got = [send(row_stat.at[1], row_in.at[2 + d], device(dy=d)) for d in (1, 2, 3)]
    col_got.wait_recv()
    col_stat[1] = join_lse([col_stat[0], col_in[0]])
    col_got = [send(col_stat.at[1], col_in.at[d], device(dz=d)) for d in range(1, NZ)]
    for copy in row_got:
        copy.wait_recv()
    row_stat[2] = join_lse([row_stat[1]] + [row_in[3 + i] for i in range(3)]) + 1.0
    for dy in range(NY):
        for dx in range(NX):
            whole = row_stat[2, pl.ds(block_row(dy, dx), 1), :]
            g0, k0 = where_is[0, dx, dy]
            g1, k1 = where_is[1, dy, dx]
            row_lse[g0, k0 : k0 + 1, :] = whole
            row_lse[g1, k1 : k1 + 1, :] = whole
    for copy in col_got:
        copy.wait_recv()
    col_stat[2] = join_lse([col_stat[1]] + [col_in[d] for d in range(1, NZ)]) + 1.0
    for tile in range(8):
        c = slice(tile * 128, tile * 128 + 128)
        first, second = TEXT_BLOCKS[2 * tile : 2 * tile + 2]
        line0 = col_stat[2, pl.ds(text_place(*first), 1), :]
        line1 = col_stat[2, pl.ds(text_place(*second), 1), :]
        col_lse[0:1, c] = jnp.where(low, line0, pltpu.roll(line1, 64, 1))
        col_lse[1:2, c] = jnp.where(low, pltpu.roll(line0, 64, 1), line1)

    @pl.loop(0, 8)
    def _(g):
        r = pl.multiple_of(g * 128, 128)
        lines = jnp.broadcast_to(row_lse[g][:, None, :], (4, 32, 128)).reshape(128, 128)
        learn_row = jnp.sum(jnp.where(learn_spot, lines, 0.0), axis=1, keepdims=True)
        teach_row = jnp.sum(jnp.where(teach_spot, lines, 0.0), axis=1, keepdims=True)
        for tg in range(4):
            c = slice(tg * 256, tg * 256 + 256)
            s, t = learn[pl.ds(r, 128), c], teach[pl.ds(r, 128), c]
            value = (jnp.exp2(s - learn_row) - jnp.exp2(t - teach_row)) + (
                jnp.exp2(s - col_lse[0:1, c]) - jnp.exp2(t - col_lse[1:2, c])
            )
            weight[pl.ds(r, 128), c] = value.astype(BF16)

    text_got = []

    def text_grads(*tiles):
        for tile in tiles:
            c = slice(tile * 128, tile * 128 + 128)
            part = tn_dot(weight[:, c], img[:, :ds]) * grad_scale
            for i, (k, sib) in enumerate(TEXT_BLOCKS[2 * tile : 2 * tile + 2]):
                piece = part[i * 64 : i * 64 + 64, :]
                if sib:
                    text_send[k] = piece.astype(BF16)
                    text_got.append(send(text_send.at[k], text_in.at[k], device(sibling=True)))
                else:
                    text_own[k] = piece

    text_grads(0, 2, 4, 6, 7)
    for g, keys in enumerate(HALF_BLOCKS):
        part = jnp.dot(weight[g * 128 : g * 128 + 128, :], txt[:, :ds], preferred_element_type=F32) * grad_scale
        for k, (h, p, q) in enumerate(keys):
            piece = part[k * 32 : k * 32 + 32, :]
            if q == 0:
                image_own[h, p * 32 : p * 32 + 32, :] = piece
            else:
                image_send[h, q - 1, p * 32 : p * 32 + 32, :] = piece.astype(BF16)
    image_got = [
        [send(image_send.at[h, q - 1], image_in.at[h, q - 1], along(h, 2, q)) for q in (1, 2, 3)] for h in (0, 1)
    ]
    text_grads(1, 3, 5)
    for copy in text_got:
        copy.wait_recv()
    for k in range(NZ):
        text_own[k] = text_own[k] + text_in[k].astype(F32)
    for i, k in enumerate((1, 7, 3, 5, 4)):
        text_send2[i] = text_own[k].astype(BF16)
    merge = [
        send(text_send2.at[2], text_in2.at[2], device(dz=1)),
        send(text_send2.at[4, pl.ds(0, 32)], text_in2.at[4, pl.ds(0, 32)], device(dz=2)),
        send(text_send2.at[3], text_in2.at[3], device(dz=-1)),
        send(text_send2.at[4, pl.ds(32, 32)], text_in2.at[4, pl.ds(32, 32)], device(dz=-2)),
    ]
    final = [
        send(text_send2.at[0], text_in2.at[0], device(dz=1)),
        send(text_send2.at[1], text_in2.at[1], device(dz=-1)),
    ]
    for h in (0, 1):
        for copy in image_got[h]:
            copy.wait_recv()
        image_sum[h] = image_own[h] + functools.reduce(jnp.add, [image_in[h, i].astype(F32) for i in range(3)])
        image_send2[h] = image_sum[h, 32:128, :].astype(BF16)
    image_got = []
    for h in (0, 1):
        for p in (1, 2, 3):
            at = pl.ds((p - 1) * 32, 32)
            image_got.append(send(image_send2.at[h, at], image_in2.at[h, at], along(h, 1, p)))
    for copy in merge:
        copy.wait_recv()
    for i, k, h in ((0, 2, 0), (1, 6, 1)):
        joined = text_own[k] + text_in2[2 + i].astype(F32)
        near = slice(h * 32, h * 32 + 32)
        far = slice(32 - h * 32, 64 - h * 32)
        text_send3[i, near, :] = (joined[near] + text_in2[4, near, :].astype(F32)).astype(BF16)
        text_send3[i, far, :] = joined[far].astype(BF16)
        final.append(send(text_send3.at[i], text_in3.at[i], device(dz=2 - 4 * i)))
    for copy in image_got:
        copy.wait_recv()
    for h in (0, 1):
        at = slice(h * 32, h * 32 + 32)
        total = image_sum[h, 0:32, :] + functools.reduce(
            jnp.add, [image_in2[h, i * 32 : i * 32 + 32, :].astype(F32) for i in range(3)]
        )
        image_out[at, :] = back_norm(total, si_ref[at, :])
    for copy in final:
        copy.wait_recv()
    total = text_own[0]
    for ref in (text_in2, text_in3):
        total = total + ref[0].astype(F32) + ref[1].astype(F32)
    text_out[...] = back_norm(total, st_ref[...])
    for copy in copies:
        copy.wait_send()


def body(student_image, student_text, teacher_image, teacher_text, teacher_scale, student_scale):
    own, ds = student_image.shape
    width = ds + teacher_image.shape[1]
    vmem = pl.BlockSpec(memory_space=pltpu.VMEM)
    smem = pl.BlockSpec(memory_space=pltpu.SMEM)
    hbm = pl.BlockSpec(memory_space=pltpu.HBM)
    out = jax.ShapeDtypeStruct((own, ds), F32)
    return pl.pallas_call(
        kernel,
        out_shape=(out, out),
        in_specs=[smem, smem, hbm, hbm, hbm, hbm],
        out_specs=(vmem, vmem),
        scratch_shapes=[
            pltpu.VMEM((own, ds), BF16),
            pltpu.VMEM((own, ds), BF16),
            pltpu.VMEM((own, width - ds), BF16),
            pltpu.VMEM((own, width - ds), BF16),
            pltpu.VMEM((1024, width), BF16),
            pltpu.VMEM((1024, width), BF16),
            pltpu.VMEM((1024, 1024), F32),
            pltpu.VMEM((1024, 1024), F32),
            pltpu.VMEM((1024, 1024), BF16),
            pltpu.VMEM((4, 8, 4, 128), F32),
            pltpu.VMEM((8, 2, 1024), F32),
            pltpu.VMEM((3, 16, 128), F32),
            pltpu.VMEM((3, 16, 128), F32),
            pltpu.VMEM((6, 16, 128), F32),
            pltpu.VMEM((8, 16, 128), F32),
            pltpu.VMEM((8, 4, 128), F32),
            pltpu.VMEM((2, 1024), F32),
            pltpu.VMEM((2, 128, ds), F32),
            pltpu.VMEM((2, 3, 128, ds), BF16),
            pltpu.VMEM((2, 3, 128, ds), BF16),
            pltpu.VMEM((2, 128, ds), F32),
            pltpu.VMEM((2, 96, ds), BF16),
            pltpu.VMEM((2, 96, ds), BF16),
            pltpu.VMEM((NZ, 64, ds), F32),
            pltpu.VMEM((NZ, 64, ds), BF16),
            pltpu.VMEM((NZ, 64, ds), BF16),
            pltpu.VMEM((5, 64, ds), BF16),
            pltpu.VMEM((5, 64, ds), BF16),
            pltpu.VMEM((2, 64, ds), BF16),
            pltpu.VMEM((2, 64, ds), BF16),
            pltpu.SemaphoreType.DMA((COPIES,)),
            pltpu.SemaphoreType.DMA((COPIES,)),
            pltpu.SemaphoreType.DMA((4,)),
        ],
        compiler_params=pltpu.CompilerParams(
            collective_id=0, has_side_effects=True, vmem_limit_bytes=48 * 1024 * 1024
        ),
    )(
        teacher_scale.reshape(1, 1), student_scale.reshape(1, 1),
        student_image, student_text, teacher_image, teacher_text,
    )


def solution(mesh):
    placed = P(("row", "col"), None)
    return jax.shard_map(
        body,
        mesh=mesh,
        in_specs=(placed, placed, placed, placed, P(), P()),
        out_specs=(placed, placed),
        check_vma=False,
    )
```

time: 91.2 us -> 71.9 us (0.79)
  Pallas kernels: 83.6 us -> 64.1 us
    pallas_call x1, Pallas kernels: 83.6 us -> 64.1 us  [body(): pl.pallas_call(kernel, out_shape=(out, out), in_specs=[smem, smem, hbm, h...]
where the time goes in v2:
time: 71.9 us; the launch traced here: 70.9 us
  Pallas kernels  64.1 us (89%)
  local copies, waits for them, and re-layouts  4.81 us (7%)
  between operations  1.94 us (3%)
    pallas_call x1, Pallas kernels, body(): pl.pallas_call(kernel, out_shape=(out, out), in_specs=[smem, smem, hbm, h...  64.1 us
    unnamed x10, local copies, waits for them, and re-layouts  4.81 us

profile of v2, /device:TPU:1, one launch (start us, length us, event | category | flops | bytes accessed | tf_op | source)
XLA Modules:
  0.0 70.9 jit_solution(10364238801153370915)
XLA Ops:
  1.9 0.0 copy-start
  1.9 0.9 %copy-done = bf16[64,1280]{1,0:T(8,128)(2,1)S(1)} copy-done((bf16[64,1280]{1,0:T(8,128)(2,1)S(1)}, bf16[64,1280]{1,0:T(8,128)(2,1)}, u32[]{:S(2)}) %copy-start) | copy-done | bytes 163864
  2.8 0.0 copy-start.1
  2.8 0.9 %copy-done.1 = bf16[64,1280]{1,0:T(8,128)(2,1)S(1)} copy-done((bf16[64,1280]{1,0:T(8,128)(2,1)S(1)}, bf16[64,1280]{1,0:T(8,128)(2,1)}, u32[]{:S(2)}) %copy-start.1) | copy-done | bytes 163864
  3.8 0.0 copy-start.2
  3.8 0.8 %copy-done.2 = bf16[64,512]{1,0:T(8,128)(2,1)S(1)} copy-done((bf16[64,512]{1,0:T(8,128)(2,1)S(1)}, bf16[64,512]{1,0:T(8,128)(2,1)}, u32[]{:S(2)}) %copy-start.2) | copy-done | bytes 65560
  4.6 0.0 copy-start.3
  4.6 0.8 %copy-done.3 = bf16[64,512]{1,0:T(8,128)(2,1)S(1)} copy-done((bf16[64,512]{1,0:T(8,128)(2,1)S(1)}, bf16[64,512]{1,0:T(8,128)(2,1)}, u32[]{:S(2)}) %copy-start.3) | copy-done | bytes 65560
  5.4 64.1 %shard_map.77 = (f32[64,512]{1,0:T(8,128)S(1)}, f32[64,512]{1,0:T(8,128)S(1)}) custom-call(f32[1,1]{1,0:T(1,128)} %bitcast.2.tscale_ref, f32[1,1]{1,0:T(1,128)} %bitcast.3.sscale_ref, bf16[64,512]{1,0:T(8,128)(2,1)S(1)} %copy-done.2, bf16[64,512]{1,0:T(8,128)(2,1)S(1)} %copy-done.3, bf16[64,1280]{1,0:T(8,128)(2,1)S(1)} %copy-done, bf16[64,1280]{1,0:T(8,128)(2,1)S(1)} %copy-done.1), custom_call_target="tpu_custom_call" | custom-call | tf_op jit(solution)/shard_map/pallas_call | solution.py:427
  69.6 0.7 copy.12
  70.2 0.7 copy.13
Async XLA Ops:
  1.9 0.9 %copy-start = (bf16[64,1280]{1,0:T(8,128)(2,1)S(1)}, bf16[64,1280]{1,0:T(8,128)(2,1)}, u32[]{:S(2)}) copy-start(bf16[64,1280]{1,0:T(8,128)(2,1)} %ti_hbm.1) | copy-start | bytes 491524
  2.8 0.9 %copy-start.1 = (bf16[64,1280]{1,0:T(8,128)(2,1)S(1)}, bf16[64,1280]{1,0:T(8,128)(2,1)}, u32[]{:S(2)}) copy-start(bf16[64,1280]{1,0:T(8,128)(2,1)} %tt_hbm.1) | copy-start | bytes 491524
  3.8 0.8 %copy-start.2 = (bf16[64,512]{1,0:T(8,128)(2,1)S(1)}, bf16[64,512]{1,0:T(8,128)(2,1)}, u32[]{:S(2)}) copy-start(bf16[64,512]{1,0:T(8,128)(2,1)} %si_hbm.1) | copy-start | bytes 196612
  4.6 0.8 %copy-start.3 = (bf16[64,512]{1,0:T(8,128)(2,1)S(1)}, bf16[64,512]{1,0:T(8,128)(2,1)}, u32[]{:S(2)}) copy-start(bf16[64,512]{1,0:T(8,128)(2,1)} %st_hbm.1) | copy-start | bytes 196612

commit v3 on v2

--- a/solution.py
+++ b/solution.py
@@ -64,7 +64,8 @@
 
 def kernel(
     tscale_ref, sscale_ref, si_hbm, st_hbm, ti_hbm, tt_hbm, image_out, text_out,
-    si_ref, st_ref, ti_ref, tt_ref, img, txt, teach, learn, weight, row_part, col_part, row_stat, col_stat, row_in, col_in, row_lse, col_lse,
+    si_ref, st_ref, ti_ref, tt_ref, img, txt, teach, learn, weight, row_part, col_part, row_stat, col_stat, row_in, col_in,
+    row_local, col_local, row_whole, row_scale, col_scale, by_row, by_col,
     image_own, image_send, image_in, image_sum, image_send2, image_in2,
     text_own, text_send, text_in, text_send2, text_in2, text_send3, text_in3,
     send_sem, recv_sem, load_sem,
@@ -195,9 +196,8 @@
             for ref, lo, hi, scale in ((learn, 0, ds, learn_scale), (teach, ds, img.shape[1], teach_scale)):
                 ref[r, c] = nt_dot(img[r, lo:hi], txt[c, lo:hi]) * scale
 
-        @pl.loop(first, last)
-        def _(g):
-            r = pl.multiple_of(g * 128, 128)
+        for g in range(first, last):
+            r = g * 128
             for b in blocks:
                 c = slice(*COLUMNS[b])
                 row_ls = []
@@ -268,128 +268,184 @@
 
     low = lax.broadcasted_iota(jnp.int32, (1, 128), 1) < 64
     half0 = lax.broadcasted_iota(jnp.int32, (1, 128), 1) % 64 < 32
-    row_local = join_lse([row_part[tg] for tg in range(4)])
-
-    def block_row(dy, dx):
-        return ((y + dy) % NY) * NX + (x + dx) % NX
-
     where_is = {key: (g, k) for g, keys in enumerate(HALF_BLOCKS) for k, key in enumerate(keys)}
-    for dy in range(NY):
-        for dx in range(NX):
-            g0, k0 = where_is[0, dx, dy]
-            g1, k1 = where_is[1, dy, dx]
-            line0, line1 = row_local[g0, k0 : k0 + 1, :], row_local[g1, k1 : k1 + 1, :]
-            row_stat[0, pl.ds(block_row(dy, dx), 1), :] = jnp.where(half0, line0, line1)
-    row_got = [send(row_stat.at[0], row_in.at[d - 1], device(dx=d)) for d in (1, 2, 3)]
-
-    col_local = join_lse([col_part[g] for g in range(8)])
-
-    def text_place(k, sib):
-        return (1 - core if sib else core) * NZ + (z + k) % NZ
-
+    row_places = [
+        (((y + dy) % NY) * NX + (x + dx) % NX, where_is[0, dx, dy], where_is[1, dy, dx])
+        for dy in range(NY)
+        for dx in range(NX)
+    ]
+    col_places = [(1 - core if sib else core) * NZ + (z + k) % NZ for k, sib in TEXT_BLOCKS]
+
+    def spread(lines):
+        lines = jnp.broadcast_to(lines[:, None, :], (4, 32, 128)).reshape(128, 128)
+        for mask in (learn_spot, teach_spot):
+            yield jnp.broadcast_to(jnp.sum(jnp.where(mask, lines, 0.0), axis=1, keepdims=True), (128, 128))
+
+    col_local[...] = join_lse([col_part[g] for g in range(8)])
     for tile in range(8):
         c = slice(tile * 128, tile * 128 + 128)
         ls, lt = col_local[0:1, c], col_local[1:2, c]
-        first, second = TEXT_BLOCKS[2 * tile : 2 * tile + 2]
-        col_stat[0, pl.ds(text_place(*first), 1), :] = jnp.where(low, ls, pltpu.roll(lt, 64, 1))
-        col_stat[0, pl.ds(text_place(*second), 1), :] = jnp.where(low, pltpu.roll(ls, 64, 1), lt)
+        first, second = col_places[2 * tile : 2 * tile + 2]
+        col_stat[0, pl.ds(first, 1), :] = jnp.where(low, ls, pltpu.roll(lt, 64, 1))
+        col_stat[0, pl.ds(second, 1), :] = jnp.where(low, pltpu.roll(ls, 64, 1), lt)
     col_got = send(col_stat.at[0], col_in.at[0], device(sibling=True))
-
+    row_local[...] = join_lse([row_part[b] for b in range(len(COLUMNS))])
+    for place, (g0, k0), (g1, k1) in row_places:
+        row_stat[0, pl.ds(place, 1), :] = jnp.where(half0, row_local[g0, k0 : k0 + 1, :], row_local[g1, k1 : k1 + 1, :])
+    row_got = [send(row_stat.at[0], row_in.at[d - 1], device(dx=d)) for d in (2, 1, 3)]
+
+    def local_softmax(*groups):
+        for g in groups:
+            r = slice(g * 128, g * 128 + 128)
+            row_ls = list(spread(row_local[g]))
+            for tile in range(8):
+                c = slice(tile * 128, tile * 128 + 128)
+                for i, ref in enumerate((learn, teach)):
+                    block = ref[r, c] - 1.0
+                    by_row[i, r, c] = jnp.exp2(block - row_ls[i])
+                    by_col[i, r, c] = jnp.exp2(block - col_local[i : i + 1, c])
+
+    local_softmax(0, 1)
+    col_got.wait_recv()
+    col_stat[1] = join_lse([col_stat[0], col_in[0]])
+    col_got = [send(col_stat.at[1], col_in.at[d], device(dz=d)) for d in (4, 3, 5, 2, 6, 1, 7)]
+    local_softmax(2, 3, 4)
     for copy in row_got:
         copy.wait_recv()
     row_stat[1] = join_lse([row_stat[0]] + [row_in[i] for i in range(3)])
-    row_got = [send(row_stat.at[1], row_in.at[2 + d], device(dy=d)) for d in (1, 2, 3)]
-    col_got.wait_recv()
-    col_stat[1] = join_lse([col_stat[0], col_in[0]])
-    col_got = [send(col_stat.at[1], col_in.at[d], device(dz=d)) for d in range(1, NZ)]
+    row_got = [send(row_stat.at[1], row_in.at[2 + d], device(dy=d)) for d in (2, 1, 3)]
+    local_softmax(5, 6, 7)
+    for copy in col_got:
+        copy.wait_recv()
+    col_stat[2] = join_lse([col_stat[1]] + [col_in[d] for d in range(1, NZ)])
+    for tile in range(8):
+        c = slice(tile * 128, tile * 128 + 128)
+        first, second = col_places[2 * tile : 2 * tile + 2]
+        line0 = col_stat[2, pl.ds(first, 1), :]
+        line1 = col_stat[2, pl.ds(second, 1), :]
+        col_scale[0:1, c] = jnp.exp2(col_local[0:1, c] - jnp.where(low, line0, pltpu.roll(line1, 64, 1)))
+        col_scale[1:2, c] = jnp.exp2(col_local[1:2, c] - jnp.where(low, pltpu.roll(line0, 64, 1), line1))
     for copy in row_got:
         copy.wait_recv()
-    row_stat[2] = join_lse([row_stat[1]] + [row_in[3 + i] for i in range(3)]) + 1.0
-    for dy in range(NY):
-        for dx in range(NX):
-            whole = row_stat[2, pl.ds(block_row(dy, dx), 1), :]
-            g0, k0 = where_is[0, dx, dy]
-            g1, k1 = where_is[1, dy, dx]
-            row_lse[g0, k0 : k0 + 1, :] = whole
-            row_lse[g1, k1 : k1 + 1, :] = whole
-    for copy in col_got:
-        copy.wait_recv()
-    col_stat[2] = join_lse([col_stat[1]] + [col_in[d] for d in range(1, NZ)]) + 1.0
-    for tile in range(8):
-        c = slice(tile * 128, tile * 128 + 128)
-        first, second = TEXT_BLOCKS[2 * tile : 2 * tile + 2]
-        line0 = col_stat[2, pl.ds(text_place(*first), 1), :]
-        line1 = col_stat[2, pl.ds(text_place(*second), 1), :]
-        col_lse[0:1, c] = jnp.where(low, line0, pltpu.roll(line1, 64, 1))
-        col_lse[1:2, c] = jnp.where(low, pltpu.roll(line0, 64, 1), line1)
-
-    @pl.loop(0, 8)
-    def _(g):
-        r = pl.multiple_of(g * 128, 128)
-        lines = jnp.broadcast_to(row_lse[g][:, None, :], (4, 32, 128)).reshape(128, 128)
-        learn_row = jnp.sum(jnp.where(learn_spot, lines, 0.0), axis=1, keepdims=True)
-        teach_row = jnp.sum(jnp.where(teach_spot, lines, 0.0), axis=1, keepdims=True)
-        for tg in range(4):
-            c = slice(tg * 256, tg * 256 + 256)
-            s, t = learn[pl.ds(r, 128), c], teach[pl.ds(r, 128), c]
-            value = (jnp.exp2(s - learn_row) - jnp.exp2(t - teach_row)) + (
-                jnp.exp2(s - col_lse[0:1, c]) - jnp.exp2(t - col_lse[1:2, c])
-            )
-            weight[pl.ds(r, 128), c] = value.astype(BF16)
-
-    text_got = []
+    row_stat[2] = join_lse([row_stat[1]] + [row_in[3 + i] for i in range(3)])
+    for place, (g0, k0), (g1, k1) in row_places:
+        whole = row_stat[2, pl.ds(place, 1), :]
+        for g, k in ((g0, k0), (g1, k1)):
+            row_whole[g, k : k + 1, :] = whole
+    for g in range(8):
+        r = slice(g * 128, g * 128 + 128)
+        row_scale[0, r, :], row_scale[1, r, :] = spread(jnp.exp2(row_local[g] - row_whole[g]))
+
+    def weights(*tiles):
+        for g in range(8):
+            r = slice(g * 128, g * 128 + 128)
+            learn_row, teach_row = row_scale[0, r, :], row_scale[1, r, :]
+            for tile in tiles:
+                c = slice(tile * 128, tile * 128 + 128)
+                value = (by_row[0, r, c] * learn_row - by_row[1, r, c] * teach_row) + (
+                    by_col[0, r, c] * col_scale[0:1, c] - by_col[1, r, c] * col_scale[1:2, c]
+                )
+                weight[r, c] = value.astype(BF16)
+
+    text_got = {}
 
     def text_grads(*tiles):
-        for tile in tiles:
-            c = slice(tile * 128, tile * 128 + 128)
-            part = tn_dot(weight[:, c], img[:, :ds]) * grad_scale
-            for i, (k, sib) in enumerate(TEXT_BLOCKS[2 * tile : 2 * tile + 2]):
-                piece = part[i * 64 : i * 64 + 64, :]
-                if sib:
-                    text_send[k] = piece.astype(BF16)
-                    text_got.append(send(text_send.at[k], text_in.at[k], device(sibling=True)))
-                else:
-                    text_own[k] = piece
-
-    text_grads(0, 2, 4, 6, 7)
-    for g, keys in enumerate(HALF_BLOCKS):
-        part = jnp.dot(weight[g * 128 : g * 128 + 128, :], txt[:, :ds], preferred_element_type=F32) * grad_scale
-        for k, (h, p, q) in enumerate(keys):
+        c = slice(tiles[0] * 128, tiles[-1] * 128 + 128)
+        part = tn_dot(weight[:, c], img[:, :ds]) * grad_scale
+        for i, (k, sib) in enumerate(TEXT_BLOCKS[2 * tiles[0] : 2 * tiles[-1] + 2]):
+            piece = part[i * 64 : i * 64 + 64, :]
+            if sib:
+                text_send[k] = piece.astype(BF16)
+                text_got[k] = send(text_send.at[k], text_in.at[k], device(sibling=True))
+            else:
+                text_own[k] = piece
+
+    def join_cores(*ks):
+        for k in ks:
+            text_got[k].wait_recv()
+            text_own[k] = text_own[k] + text_in[k].astype(F32)
+
+    image_got = {}
+
+    def image_grads(g):
+        r = slice(g * 128, g * 128 + 128)
+        part = jnp.dot(weight[r, :], txt[:, :ds], preferred_element_type=F32) * grad_scale
+        for k, (h, p, q) in enumerate(HALF_BLOCKS[g]):
             piece = part[k * 32 : k * 32 + 32, :]
             if q == 0:
                 image_own[h, p * 32 : p * 32 + 32, :] = piece
             else:
                 image_send[h, q - 1, p * 32 : p * 32 + 32, :] = piece.astype(BF16)
-    image_got = [
-        [send(image_send.at[h, q - 1], image_in.at[h, q - 1], along(h, 2, q)) for q in (1, 2, 3)] for h in (0, 1)
-    ]
-    text_grads(1, 3, 5)
-    for copy in text_got:
-        copy.wait_recv()
-    for k in range(NZ):
-        text_own[k] = text_own[k] + text_in[k].astype(F32)
-    for i, k in enumerate((1, 7, 3, 5, 4)):
+
+    def image_pass_on(q, first, last):
+        for h in (0, 1):
+            at = pl.ds(first * 32, (last - first) * 32)
+            copy = send(image_send.at[h, q - 1, at], image_in.at[h, q - 1, at], along(h, 2, q))
+            for p in range(first, last):
+                image_got[h, p, q] = copy
+
+    def join_images(*ps):
+        for p in ps:
+            at = slice(p * 32, p * 32 + 32)
+            for h in (0, 1):
+                for q in (1, 2, 3):
+                    if image_got[h, p, q] is not None:
+                        image_got[h, p, q].wait_recv()
+                        for other in range(NX):
+                            if other != p and image_got[h, other, q] is image_got[h, p, q]:
+                                image_got[h, other, q] = None
+                        image_got[h, p, q] = None
+                total = image_own[h, at, :] + functools.reduce(
+                    jnp.add, [image_in[h, i, at, :].astype(F32) for i in range(3)]
+                )
+                if p == 0:
+                    image_sum[h] = total
+                else:
+                    image_send2[h, p - 1] = total.astype(BF16)
+                    image_got2.append(send(image_send2.at[h, p - 1], image_in2.at[h, p - 1], along(h, 1, p)))
+
+    weights(6, 7)
+    text_grads(6, 7)
+    weights(5)
+    text_grads(5)
+    weights(0, 1, 2, 3, 4)
+    image_grads(7)
+    image_pass_on(2, 2, 4)
+    join_cores(3, 5, 4)
+    for i, k in ((2, 3), (3, 5), (4, 4)):
         text_send2[i] = text_own[k].astype(BF16)
     merge = [
+        send(text_send2.at[4, pl.ds(0, 32)], text_in2.at[4, pl.ds(0, 32)], device(dz=2)),
+        send(text_send2.at[4, pl.ds(32, 32)], text_in2.at[4, pl.ds(32, 32)], device(dz=-2)),
         send(text_send2.at[2], text_in2.at[2], device(dz=1)),
-        send(text_send2.at[4, pl.ds(0, 32)], text_in2.at[4, pl.ds(0, 32)], device(dz=2)),
         send(text_send2.at[3], text_in2.at[3], device(dz=-1)),
-        send(text_send2.at[4, pl.ds(32, 32)], text_in2.at[4, pl.ds(32, 32)], device(dz=-2)),
     ]
+    image_grads(6)
+    image_pass_on(2, 0, 2)
+    image_grads(5)
+    image_grads(4)
+    image_pass_on(1, 2, 4)
+    image_pass_on(3, 2, 4)
+    image_grads(3)
+    image_pass_on(1, 1, 2)
+    image_pass_on(3, 1, 2)
+    image_grads(2)
+    image_pass_on(3, 0, 1)
+    image_grads(1)
+    image_pass_on(1, 0, 1)
+    text_grads(1, 2)
+    text_grads(3, 4)
+    text_grads(0)
+    image_grads(0)
+    join_cores(1, 7)
+    for i, k in ((0, 1), (1, 7)):
+        text_send2[i] = text_own[k].astype(BF16)
     final = [
         send(text_send2.at[0], text_in2.at[0], device(dz=1)),
         send(text_send2.at[1], text_in2.at[1], device(dz=-1)),
     ]
-    for h in (0, 1):
-        for copy in image_got[h]:
-            copy.wait_recv()
-        image_sum[h] = image_own[h] + functools.reduce(jnp.add, [image_in[h, i].astype(F32) for i in range(3)])
-        image_send2[h] = image_sum[h, 32:128, :].astype(BF16)
-    image_got = []
-    for h in (0, 1):
-        for p in (1, 2, 3):
-            at = pl.ds((p - 1) * 32, 32)
-            image_got.append(send(image_send2.at[h, at], image_in2.at[h, at], along(h, 1, p)))
+    join_cores(2, 6)
+    image_got2 = []
     for copy in merge:
         copy.wait_recv()
     for i, k, h in ((0, 2, 0), (1, 6, 1)):
@@ -399,13 +455,13 @@
         text_send3[i, near, :] = (joined[near] + text_in2[4, near, :].astype(F32)).astype(BF16)
         text_send3[i, far, :] = joined[far].astype(BF16)
         final.append(send(text_send3.at[i], text_in3.at[i], device(dz=2 - 4 * i)))
-    for copy in image_got:
+    join_images(2, 3, 1, 0)
+    join_cores(0)
+    for copy in image_got2:
         copy.wait_recv()
     for h in (0, 1):
         at = slice(h * 32, h * 32 + 32)
-        total = image_sum[h, 0:32, :] + functools.reduce(
-            jnp.add, [image_in2[h, i * 32 : i * 32 + 32, :].astype(F32) for i in range(3)]
-        )
+        total = image_sum[h] + functools.reduce(jnp.add, [image_in2[h, i].astype(F32) for i in range(3)])
         image_out[at, :] = back_norm(total, si_ref[at, :])
     for copy in final:
         copy.wait_recv()
@@ -447,12 +503,17 @@
             pltpu.VMEM((8, 16, 128), F32),
             pltpu.VMEM((8, 4, 128), F32),
             pltpu.VMEM((2, 1024), F32),
+            pltpu.VMEM((8, 4, 128), F32),
+            pltpu.VMEM((2, 1024, 128), F32),
+            pltpu.VMEM((2, 1024), F32),
+            pltpu.VMEM((2, 1024, 1024), F32),
+            pltpu.VMEM((2, 1024, 1024), F32),
             pltpu.VMEM((2, 128, ds), F32),
             pltpu.VMEM((2, 3, 128, ds), BF16),
             pltpu.VMEM((2, 3, 128, ds), BF16),
-            pltpu.VMEM((2, 128, ds), F32),
-            pltpu.VMEM((2, 96, ds), BF16),
-            pltpu.VMEM((2, 96, ds), BF16),
+            pltpu.VMEM((2, 32, ds), F32),
+            pltpu.VMEM((2, 3, 32, ds), BF16),
+            pltpu.VMEM((2, 3, 32, ds), BF16),
             pltpu.VMEM((NZ, 64, ds), F32),
             pltpu.VMEM((NZ, 64, ds), BF16),
             pltpu.VMEM((NZ, 64, ds), BF16),
@@ -465,7 +526,7 @@
             pltpu.SemaphoreType.DMA((4,)),
         ],
         compiler_params=pltpu.CompilerParams(
-            collective_id=0, has_side_effects=True, vmem_limit_bytes=48 * 1024 * 1024
+            collective_id=0, has_side_effects=True, vmem_limit_bytes=60 * 1024 * 1024
         ),
     )(
         teacher_scale.reshape(1, 1), student_scale.reshape(1, 1),

time: 71.9 us -> 63.5 us (0.88); the launches traced: 70.9 us -> 63.3 us
  Pallas kernels: 64.1 us -> 59.1 us
  local copies, waits for them, and re-layouts: 4.81 us -> 2.26 us
    pallas_call x1, Pallas kernels: 64.1 us -> 59.1 us  [body(): pl.pallas_call(kernel, out_shape=(out, out), in_specs=[smem, smem, hbm, h...]
    unnamed x10 -> x4, local copies, waits for them, and re-layouts: 4.81 us -> 2.26 us
where the time goes in v3:
time: 63.5 us; the launch traced here: 63.3 us
  Pallas kernels  59.1 us (93%)
  local copies, waits for them, and re-layouts  2.26 us (4%)
  between operations  1.94 us (3%)
    pallas_call x1, Pallas kernels, body(): pl.pallas_call(kernel, out_shape=(out, out), in_specs=[smem, smem, hbm, h...  59.1 us
    unnamed x4, local copies, waits for them, and re-layouts  2.26 us

profile of v3, /device:TPU:1, one launch (start us, length us, event | category | flops | bytes accessed | tf_op | source)
XLA Modules:
  0.0 63.3 jit_solution(15363611734094170682)
XLA Ops:
  1.9 59.1 %shard_map.77 = (f32[64,512]{1,0:T(8,128)}, f32[64,512]{1,0:T(8,128)}) custom-call(f32[1,1]{1,0:T(1,128)} %bitcast.2.tscale_ref, f32[1,1]{1,0:T(1,128)} %bitcast.3.sscale_ref, bf16[64,512]{1,0:T(8,128)(2,1)} %si_hbm.1, bf16[64,512]{1,0:T(8,128)(2,1)} %st_hbm.1, bf16[64,1280]{1,0:T(8,128)(2,1)} %ti_hbm.1, bf16[64,1280]{1,0:T(8,128)(2,1)} %tt_hbm.1), custom_call_target="tpu_custom_call" | custom-call | tf_op jit(solution)/shard_map/pallas_call | solution.py:483
  61.1 0.0 copy-start
  61.1 1.6 %copy.12 = f32[64,512]{1,0:T(8,128)} copy(f32[64,512]{1,0:T(8,128)} %get-tuple-element.4) | data formatting | bytes 262144
  62.7 0.0 copy-done
  62.7 0.7 %copy.13 = f32[64,512]{1,0:T(8,128)} copy(f32[64,512]{1,0:T(8,128)S(1)} %copy-done) | data formatting | bytes 262144
Async XLA Ops:
  61.1 1.6 %copy-start = (f32[64,512]{1,0:T(8,128)S(1)}, f32[64,512]{1,0:T(8,128)}, u32[]{:S(2)}) copy-start(f32[64,512]{1,0:T(8,128)} %get-tuple-element.5) | copy-start | bytes 393220

commit v4 on v3

--- a/solution.py
+++ b/solution.py
@@ -13,7 +13,7 @@
 NX, NY, NZ = 4, 4, 8
 LOG2E = math.log2(math.e)
 F32, BF16 = jnp.float32, jnp.bfloat16
-COPIES = 160
+SEMAPHORES = 64
 
 PAIRS = (
     ((0, 0), (1, 0)),
@@ -63,12 +63,12 @@
 
 
 def kernel(
-    tscale_ref, sscale_ref, si_hbm, st_hbm, ti_hbm, tt_hbm, image_out, text_out,
+    tscale_ref, sscale_ref, si_hbm, st_hbm, ti_hbm, tt_hbm, grads_out,
     si_ref, st_ref, ti_ref, tt_ref, img, txt, teach, learn, weight, row_part, col_part, row_stat, col_stat, row_in, col_in,
     row_local, col_local, row_whole, row_scale, col_scale, by_row, by_col,
     image_own, image_send, image_in, image_sum, image_send2, image_in2,
     text_own, text_send, text_in, text_send2, text_in2, text_send3, text_in3,
-    send_sem, recv_sem, load_sem,
+    sem,
 ):
     ds = si_ref.shape[1]
     row, col = lax.axis_index("row"), lax.axis_index("col")
@@ -82,30 +82,33 @@
     def along(half, axis, d):
         return device(dx=d) if (half == 0) == (axis == 1) else device(dy=d)
 
-    copies = []
-
-    def send(src, dst, target):
-        i = len(copies)
-        copy = pltpu.make_async_remote_copy(
-            src_ref=src, dst_ref=dst, send_sem=send_sem.at[i], recv_sem=recv_sem.at[i],
+    names = []
+
+    def semaphore(*name):
+        if name not in names:
+            names.append(name)
+        return sem.at[names.index(name)]
+
+    def send(src, dst, target, leaves, lands):
+        pltpu.make_async_remote_copy(
+            src_ref=src, dst_ref=dst, send_sem=semaphore("leaves", leaves), recv_sem=semaphore(*lands),
             device_id=target, device_id_type=MESH,
-        )
-        copy.start()
-        copies.append(copy)
-        return copy
-
+        ).start()
+
+    def wait(ref, *name):
+        pltpu.make_async_copy(ref, ref, semaphore(*name)).wait()
+
+    loads = [
+        pltpu.make_async_copy(src, dst, semaphore("load", i))
+        for i, (src, dst) in enumerate(((tt_hbm, tt_ref), (st_hbm, st_ref), (ti_hbm, ti_ref), (si_hbm, si_ref)))
+    ]
+    for load in loads:
+        load.start()
     barrier = pltpu.get_barrier_semaphore()
     peers = [device(dx=1), device(dx=-1), device(dy=1), device(dy=-1), device(dz=1), device(dz=-1)]
     peers += [device(sibling=True)]
     for peer in peers:
         pl.semaphore_signal(barrier, inc=1, device_id=peer, device_id_type=MESH)
-
-    loads = [
-        pltpu.make_async_copy(src, dst, load_sem.at[i])
-        for i, (src, dst) in enumerate(((ti_hbm, ti_ref), (tt_hbm, tt_ref), (si_hbm, si_ref), (st_hbm, st_ref)))
-    ]
-    for load in loads:
-        load.start()
     for load in loads:
         load.wait()
 
@@ -119,8 +122,6 @@
 
     pl.semaphore_wait(barrier, len(peers))
 
-    got = {}
-
     def rows(ref, at, size):
         return ref.at[pl.ds(at, size), :]
 
@@ -131,58 +132,53 @@
         at = IMAGE_ROW[(h, p, q)]
         return rows(img, at, 32) if part is None else rows(img, at + part * 16, 16)
 
+    def image_on(h, p, q, to, axis, d, lands, part=None):
+        send(image_rows(h, p, q, part), image_rows(h, *to, part), along(h, axis, d), "image", lands)
+
     def to_second_axis(h, p):
-        got[h, p, 1] = send(image_rows(h, p, 0), image_rows(h, p, 1), along(h, 2, -1))
-        got[h, p, 3] = send(image_rows(h, p, 0), image_rows(h, p, 3), along(h, 2, 1))
-
-    def text_send_on(k, j, part, d):
-        got["t", j, part] = send(text_rows(k, part), text_rows(j, part), device(dz=d))
-
-    def text_to_sibling(k, half):
-        got["s", k, half] = send(text_rows(k, half, 32), text_rows(k, half, 32, 1), device(sibling=True))
+        image_on(h, p, 0, (p, 1), 2, -1, ("image", p, 1))
+        image_on(h, p, 0, (p, 3), 2, 1, ("image", p, 3))
+
+    def text_on(k, j, part, d, lands):
+        send(text_rows(k, part), text_rows(j, part), device(dz=d), "text", lands)
+
+    def text_to_sibling(k, half, lands):
+        send(text_rows(k, half, 32), text_rows(k, half, 32, 1), device(sibling=True), "text", ("sibling", lands))
 
     def text_arrive(k, step):
+        wait(rows(txt, 0, 32), "text", k, step)
         for slot, part, d in ((k, step, -1), (NZ - k, 3 - step, 1)):
-            got["t", slot, part].wait_recv()
             if k < 3 or step < 2:
-                text_send_on(slot, slot - d if k < 3 else 4, part, d)
+                text_on(slot, slot - d if k < 3 else 4, part, d, ("text", k + 1, step))
             if step % 2:
-                text_to_sibling(slot, part // 2)
+                text_to_sibling(slot, part // 2, k if k > 1 else 0)
 
     def text_arrive_last(step):
-        for part in (step, 3 - step):
-            got["t", 4, part].wait_recv()
-            if step % 2:
-                text_to_sibling(4, part // 2)
-
-    def sibling_arrive(*ks):
-        for k in ks:
+        wait(rows(txt, 0, 32), "text", 4, step)
+        if step == 1:
             for half in (0, 1):
-                got["s", k, half].wait_recv()
+                text_to_sibling(4, half, 4)
+
+    def sibling_arrive(first, blocks):
+        wait(rows(txt, 0, blocks * 64), "sibling", first)
 
     def first_axis_arrive():
-        for h in (0, 1):
-            for p, part, d in ((1, 0, -1), (3, 1, 1)):
-                got[h, p, 0].wait_recv()
-                got[h, 2, 0, part] = send(image_rows(h, p, 0, part), image_rows(h, 2, 0, part), along(h, 1, d))
+        for p, part, d in ((1, 0, -1), (3, 1, 1)):
+            wait(rows(img, 0, 64), "image", p, 0)
+            for h in (0, 1):
+                image_on(h, p, 0, (2, 0), 1, d, ("image", 2, 0), part)
         for p in (1, 3):
             for h in (0, 1):
                 to_second_axis(h, p)
 
     def second_axis_arrive(p):
-        for h in (0, 1):
-            for q, part, d in ((1, 0, -1), (3, 1, 1)):
-                got[h, p, q].wait_recv()
-                got[h, p, 2, part] = send(image_rows(h, p, q, part), image_rows(h, p, 2, part), along(h, 2, d))
-
-    def last_arrive(p, q):
-        for h in (0, 1):
-            for part in (0, 1):
-                got[h, p, q, part].wait_recv()
+        for q, part, d in ((1, 0, -1), (3, 1, 1)):
+            wait(rows(img, 0, 64), "image", p, q)
+            for h in (0, 1):
+                image_on(h, p, q, (p, 2), 2, d, ("image", "last"), part)
 
     teach_scale = tscale_ref[0, 0] * LOG2E
     learn_scale = sscale_ref[0, 0] * LOG2E
-    grad_scale = sscale_ref[0, 0]
     lane = lax.broadcasted_iota(jnp.int32, (128, 128), 1)
     line = lax.broadcasted_iota(jnp.int32, (128, 128), 0)
     spot = line % 32 + 32 * (line // 64)
@@ -213,16 +209,16 @@
                 row_part[b, g] = jnp.sum(packed.reshape(4, 32, 128), axis=1)
 
     for step in range(4):
-        text_send_on(0, 1, step, -1)
-        text_send_on(0, 7, 3 - step, 1)
+        text_on(0, 1, step, -1, ("text", 1, step))
+        text_on(0, 7, 3 - step, 1, ("text", 1, step))
         if step == 0:
             for h in (0, 1):
-                got[h, 1, 0] = send(image_rows(h, 0, 0), image_rows(h, 1, 0), along(h, 1, -1))
-                got[h, 3, 0] = send(image_rows(h, 0, 0), image_rows(h, 3, 0), along(h, 1, 1))
+                image_on(h, 0, 0, (1, 0), 1, -1, ("image", 1, 0))
+                image_on(h, 0, 0, (3, 0), 1, 1, ("image", 3, 0))
     for h in (0, 1):
         to_second_axis(h, 0)
     for half in (0, 1):
-        text_to_sibling(0, half)
+        text_to_sibling(0, half, 0)
 
     text_arrive(1, 0)
     first_axis_arrive()
@@ -230,11 +226,11 @@
     text_arrive(1, 2)
     text_arrive(1, 3)
     second_axis_arrive(0)
-    last_arrive(2, 0)
+    wait(rows(img, 0, 64), "image", 2, 0)
     for h in (0, 1):
         to_second_axis(h, 2)
     text_arrive(2, 0)
-    sibling_arrive(0, 1, 7)
+    sibling_arrive(0, 3)
     logits(0, 3, 0)
     text_arrive(2, 1)
     second_axis_arrive(1)
@@ -244,7 +240,7 @@
     second_axis_arrive(3)
     text_arrive(3, 0)
     logits(4, 5, 0)
-    sibling_arrive(2, 6)
+    sibling_arrive(2, 2)
     logits(0, 3, 1)
     text_arrive(3, 1)
     logits(3, 5, 1)
@@ -253,17 +249,12 @@
     text_arrive(3, 3)
     logits(5, 6, 0, 1)
     text_arrive_last(0)
-    last_arrive(0, 2)
-    last_arrive(1, 2)
-    sibling_arrive(3, 5)
-    logits(6, 7, 0, 1)
-    logits(0, 4, 2)
+    sibling_arrive(3, 2)
+    logits(0, 6, 2)
     text_arrive_last(1)
-    logits(4, 7, 2)
-    last_arrive(3, 2)
-    last_arrive(2, 2)
-    logits(7, 8, 0, 1, 2)
-    sibling_arrive(4)
+    wait(rows(img, 0, 256), "image", "last")
+    logits(6, 8, 0, 1, 2)
+    sibling_arrive(4, 1)
     logits(0, 8, 3)
 
     low = lax.broadcasted_iota(jnp.int32, (1, 128), 1) < 64
@@ -288,11 +279,12 @@
         first, second = col_places[2 * tile : 2 * tile + 2]
         col_stat[0, pl.ds(first, 1), :] = jnp.where(low, ls, pltpu.roll(lt, 64, 1))
         col_stat[0, pl.ds(second, 1), :] = jnp.where(low, pltpu.roll(ls, 64, 1), lt)
-    col_got = send(col_stat.at[0], col_in.at[0], device(sibling=True))
+    send(col_stat.at[0], col_in.at[0], device(sibling=True), "cols", ("col", 0))
     row_local[...] = join_lse([row_part[b] for b in range(len(COLUMNS))])
     for place, (g0, k0), (g1, k1) in row_places:
         row_stat[0, pl.ds(place, 1), :] = jnp.where(half0, row_local[g0, k0 : k0 + 1, :], row_local[g1, k1 : k1 + 1, :])
-    row_got = [send(row_stat.at[0], row_in.at[d - 1], device(dx=d)) for d in (2, 1, 3)]
+    for d in (2, 1, 3):
+        send(row_stat.at[0], row_in.at[d - 1], device(dx=d), "rows", ("row", 0))
 
     def local_softmax(*groups):
         for g in groups:
@@ -306,17 +298,17 @@
                     by_col[i, r, c] = jnp.exp2(block - col_local[i : i + 1, c])
 
     local_softmax(0, 1)
-    col_got.wait_recv()
+    wait(col_in.at[0], "col", 0)
     col_stat[1] = join_lse([col_stat[0], col_in[0]])
-    col_got = [send(col_stat.at[1], col_in.at[d], device(dz=d)) for d in (4, 3, 5, 2, 6, 1, 7)]
+    for d in (4, 3, 5, 2, 6, 1, 7):
+        send(col_stat.at[1], col_in.at[d], device(dz=d), "cols", ("col", 1))
     local_softmax(2, 3, 4)
-    for copy in row_got:
-        copy.wait_recv()
+    wait(row_in.at[pl.ds(0, 3)], "row", 0)
     row_stat[1] = join_lse([row_stat[0]] + [row_in[i] for i in range(3)])
-    row_got = [send(row_stat.at[1], row_in.at[2 + d], device(dy=d)) for d in (2, 1, 3)]
+    for d in (2, 1, 3):
+        send(row_stat.at[1], row_in.at[2 + d], device(dy=d), "rows", ("row", 1))
     local_softmax(5, 6, 7)
-    for copy in col_got:
-        copy.wait_recv()
+    wait(col_in.at[pl.ds(1, NZ - 1)], "col", 1)
     col_stat[2] = join_lse([col_stat[1]] + [col_in[d] for d in range(1, NZ)])
     for tile in range(8):
         c = slice(tile * 128, tile * 128 + 128)
@@ -325,8 +317,7 @@
         line1 = col_stat[2, pl.ds(second, 1), :]
         col_scale[0:1, c] = jnp.exp2(col_local[0:1, c] - jnp.where(low, line0, pltpu.roll(line1, 64, 1)))
         col_scale[1:2, c] = jnp.exp2(col_local[1:2, c] - jnp.where(low, pltpu.roll(line0, 64, 1), line1))
-    for copy in row_got:
-        copy.wait_recv()
+    wait(row_in.at[pl.ds(3, 3)], "row", 1)
     row_stat[2] = join_lse([row_stat[1]] + [row_in[3 + i] for i in range(3)])
     for place, (g0, k0), (g1, k1) in row_places:
         whole = row_stat[2, pl.ds(place, 1), :]
@@ -347,29 +338,27 @@
                 )
                 weight[r, c] = value.astype(BF16)
 
-    text_got = {}
-
     def text_grads(*tiles):
         c = slice(tiles[0] * 128, tiles[-1] * 128 + 128)
-        part = tn_dot(weight[:, c], img[:, :ds]) * grad_scale
+        part = tn_dot(weight[:, c], img[:, :ds])
         for i, (k, sib) in enumerate(TEXT_BLOCKS[2 * tiles[0] : 2 * tiles[-1] + 2]):
             piece = part[i * 64 : i * 64 + 64, :]
             if sib:
                 text_send[k] = piece.astype(BF16)
-                text_got[k] = send(text_send.at[k], text_in.at[k], device(sibling=True))
+                lands = ("joined", min(k, NZ - k))
+                send(text_send.at[k], text_in.at[k], device(sibling=True), "joined", lands)
             else:
                 text_own[k] = piece
 
     def join_cores(*ks):
+        for first in sorted({min(k, NZ - k) for k in ks}):
+            wait(text_in.at[pl.ds(0, 1 if first in (0, 4) else 2)], "joined", first)
         for k in ks:
-            text_got[k].wait_recv()
             text_own[k] = text_own[k] + text_in[k].astype(F32)
-
-    image_got = {}
 
     def image_grads(g):
         r = slice(g * 128, g * 128 + 128)
-        part = jnp.dot(weight[r, :], txt[:, :ds], preferred_element_type=F32) * grad_scale
+        part = jnp.dot(weight[r, :], txt[:, :ds], preferred_element_type=F32)
         for k, (h, p, q) in enumerate(HALF_BLOCKS[g]):
             piece = part[k * 32 : k * 32 + 32, :]
             if q == 0:
@@ -378,23 +367,15 @@
                 image_send[h, q - 1, p * 32 : p * 32 + 32, :] = piece.astype(BF16)
 
     def image_pass_on(q, first, last):
+        at = pl.ds(first * 32, (last - first) * 32)
         for h in (0, 1):
-            at = pl.ds(first * 32, (last - first) * 32)
-            copy = send(image_send.at[h, q - 1, at], image_in.at[h, q - 1, at], along(h, 2, q))
-            for p in range(first, last):
-                image_got[h, p, q] = copy
-
-    def join_images(*ps):
-        for p in ps:
+            send(image_send.at[h, q - 1, at], image_in.at[h, q - 1, at], along(h, 2, q), "parts", ("parts", first))
+
+    def join_images(first, last):
+        wait(image_in.at[:, :, pl.ds(first * 32, (last - first) * 32)], "parts", first)
+        for p in range(first, last):
             at = slice(p * 32, p * 32 + 32)
             for h in (0, 1):
-                for q in (1, 2, 3):
-                    if image_got[h, p, q] is not None:
-                        image_got[h, p, q].wait_recv()
-                        for other in range(NX):
-                            if other != p and image_got[h, other, q] is image_got[h, p, q]:
-                                image_got[h, other, q] = None
-                        image_got[h, p, q] = None
                 total = image_own[h, at, :] + functools.reduce(
                     jnp.add, [image_in[h, i, at, :].astype(F32) for i in range(3)]
                 )
@@ -402,7 +383,10 @@
                     image_sum[h] = total
                 else:
                     image_send2[h, p - 1] = total.astype(BF16)
-                    image_got2.append(send(image_send2.at[h, p - 1], image_in2.at[h, p - 1], along(h, 1, p)))
+                    send(image_send2.at[h, p - 1], image_in2.at[h, p - 1], along(h, 1, p), "sums", ("sums",))
+
+    def text_pass_on(src, dst, d, lands):
+        send(src, dst, device(dz=d), "text sums", (lands,))
 
     weights(6, 7)
     text_grads(6, 7)
@@ -414,21 +398,21 @@
     join_cores(3, 5, 4)
     for i, k in ((2, 3), (3, 5), (4, 4)):
         text_send2[i] = text_own[k].astype(BF16)
-    merge = [
-        send(text_send2.at[4, pl.ds(0, 32)], text_in2.at[4, pl.ds(0, 32)], device(dz=2)),
-        send(text_send2.at[4, pl.ds(32, 32)], text_in2.at[4, pl.ds(32, 32)], device(dz=-2)),
-        send(text_send2.at[2], text_in2.at[2], device(dz=1)),
-        send(text_send2.at[3], text_in2.at[3], device(dz=-1)),
-    ]
-    image_grads(6)
-    image_pass_on(2, 0, 2)
+    for h, d in ((0, 2), (1, -2)):
+        at = pl.ds(h * 32, 32)
+        text_pass_on(text_send2.at[4, at], text_in2.at[4, at], d, "merge")
+    text_pass_on(text_send2.at[2], text_in2.at[2], 1, "merge")
+    text_pass_on(text_send2.at[3], text_in2.at[3], -1, "merge")
     image_grads(5)
     image_grads(4)
     image_pass_on(1, 2, 4)
     image_pass_on(3, 2, 4)
+    image_grads(6)
+    image_pass_on(2, 1, 2)
     image_grads(3)
     image_pass_on(1, 1, 2)
     image_pass_on(3, 1, 2)
+    image_pass_on(2, 0, 1)
     image_grads(2)
     image_pass_on(3, 0, 1)
     image_grads(1)
@@ -440,37 +424,39 @@
     join_cores(1, 7)
     for i, k in ((0, 1), (1, 7)):
         text_send2[i] = text_own[k].astype(BF16)
-    final = [
-        send(text_send2.at[0], text_in2.at[0], device(dz=1)),
-        send(text_send2.at[1], text_in2.at[1], device(dz=-1)),
-    ]
+    text_pass_on(text_send2.at[0], text_in2.at[0], 1, "final")
+    text_pass_on(text_send2.at[1], text_in2.at[1], -1, "final")
     join_cores(2, 6)
-    image_got2 = []
-    for copy in merge:
-        copy.wait_recv()
+    join_cores(0)
+    wait(text_in2.at[pl.ds(2, 3)], "merge")
     for i, k, h in ((0, 2, 0), (1, 6, 1)):
         joined = text_own[k] + text_in2[2 + i].astype(F32)
         near = slice(h * 32, h * 32 + 32)
         far = slice(32 - h * 32, 64 - h * 32)
         text_send3[i, near, :] = (joined[near] + text_in2[4, near, :].astype(F32)).astype(BF16)
         text_send3[i, far, :] = joined[far].astype(BF16)
-        final.append(send(text_send3.at[i], text_in3.at[i], device(dz=2 - 4 * i)))
-    join_images(2, 3, 1, 0)
-    join_cores(0)
-    for copy in image_got2:
-        copy.wait_recv()
+        text_pass_on(text_send3.at[i], text_in3.at[i], 2 - 4 * i, "final")
+    join_images(2, 4)
+    join_images(1, 2)
+    join_images(0, 1)
+    wait(image_in2, "sums")
     for h in (0, 1):
         at = slice(h * 32, h * 32 + 32)
         total = image_sum[h] + functools.reduce(jnp.add, [image_in2[h, i].astype(F32) for i in range(3)])
-        image_out[at, :] = back_norm(total, si_ref[at, :])
-    for copy in final:
-        copy.wait_recv()
+        grads_out[0, at, :] = back_norm(total, si_ref[at, :])
+    wait(text_in.at[pl.ds(0, 4)], "final")
     total = text_own[0]
     for ref in (text_in2, text_in3):
         total = total + ref[0].astype(F32) + ref[1].astype(F32)
-    text_out[...] = back_norm(total, st_ref[...])
-    for copy in copies:
-        copy.wait_send()
+    grads_out[1] = back_norm(total, st_ref[...])
+    wait(rows(img, 0, 960), "leaves", "image")
+    wait(rows(txt, 0, 960), "leaves", "text")
+    wait(row_in, "leaves", "rows")
+    wait(col_in, "leaves", "cols")
+    wait(image_send, "leaves", "parts")
+    wait(image_send2, "leaves", "sums")
+    wait(text_send, "leaves", "joined")
+    wait(text_send.at[pl.ds(0, 7)], "leaves", "text sums")
 
 
 def body(student_image, student_text, teacher_image, teacher_text, teacher_scale, student_scale):
@@ -479,12 +465,11 @@
     vmem = pl.BlockSpec(memory_space=pltpu.VMEM)
     smem = pl.BlockSpec(memory_space=pltpu.SMEM)
     hbm = pl.BlockSpec(memory_space=pltpu.HBM)
-    out = jax.ShapeDtypeStruct((own, ds), F32)
-    return pl.pallas_call(
+    grads = pl.pallas_call(
         kernel,
-        out_shape=(out, out),
+        out_shape=jax.ShapeDtypeStruct((2, own, ds), F32),
         in_specs=[smem, smem, hbm, hbm, hbm, hbm],
-        out_specs=(vmem, vmem),
+        out_specs=vmem,
         scratch_shapes=[
             pltpu.VMEM((own, ds), BF16),
             pltpu.VMEM((own, ds), BF16),
@@ -521,9 +506,7 @@
             pltpu.VMEM((5, 64, ds), BF16),
             pltpu.VMEM((2, 64, ds), BF16),
             pltpu.VMEM((2, 64, ds), BF16),
-            pltpu.SemaphoreType.DMA((COPIES,)),
-            pltpu.SemaphoreType.DMA((COPIES,)),
-            pltpu.SemaphoreType.DMA((4,)),
+            pltpu.SemaphoreType.DMA((SEMAPHORES,)),
         ],
         compiler_params=pltpu.CompilerParams(
             collective_id=0, has_side_effects=True, vmem_limit_bytes=60 * 1024 * 1024
@@ -532,6 +515,7 @@
         teacher_scale.reshape(1, 1), student_scale.reshape(1, 1),
         student_image, student_text, teacher_image, teacher_text,
     )
+    return grads[0] * student_scale, grads[1] * student_scale
 
 
 def solution(mesh):

time: 63.5 us -> 59.2 us (0.932)
  Pallas kernels: 59.1 us -> 55.5 us
  local copies, waits for them, and re-layouts: 2.26 us -> 0 us
  other arithmetic: 0 us -> 1.69 us
    pallas_call x1, Pallas kernels: 59.1 us -> 55.5 us  [body(): pl.pallas_call(kernel, out_shape=jax.ShapeDtypeStruct((2, own, ds), F32),...]
    unnamed x4 -> x0, local copies, waits for them, and re-layouts: 2.26 us -> none
    mul x0 -> x1, other arithmetic: none -> 1.69 us  [body(): return (grads[0] * student_scale, grads[1] * student_scale)]
where the time goes in v4:
time: 59.2 us; the launch traced here: 59.1 us
  Pallas kernels  55.5 us (94%)
  between operations  1.93 us (3%)
  other arithmetic  1.69 us (3%)
    pallas_call x1, Pallas kernels, body(): pl.pallas_call(kernel, out_shape=jax.ShapeDtypeStruct((2, own, ds), F32),...  55.5 us
    mul x1, other arithmetic, body(): return (grads[0] * student_scale, grads[1] * student_scale)  1.69 us

profile of v4, /device:TPU:1, one launch (start us, length us, event | category | flops | bytes accessed | tf_op | source)
XLA Modules:
  0.0 59.1 jit_solution(4172084067862796967)
XLA Ops:
  1.9 55.5 %shard_map.77 = f32[2,64,512]{2,1,0:T(8,128)} custom-call(f32[1,1]{1,0:T(1,128)} %bitcast.6.tscale_ref, f32[1,1]{1,0:T(1,128)} %bitcast.7.sscale_ref, bf16[64,512]{1,0:T(8,128)(2,1)} %si_hbm.1, bf16[64,512]{1,0:T(8,128)(2,1)} %st_hbm.1, bf16[64,1280]{1,0:T(8,128)(2,1)} %ti_hbm.1, bf16[64,1280]{1,0:T(8,128)(2,1)} %tt_hbm.1), custom_call_target="tpu_custom_call" | custom-call | tf_op jit(solution)/shard_map/pallas_call | solution.py:468
  57.4 1.7 %multiply_bitcast_fusion = (f32[64,512]{1,0:T(8,128)}, f32[64,512]{1,0:T(8,128)}) fusion(f32[2,64,512]{2,1,0:T(8,128)} %shard_map.77, f32[]{:T(128)} %copy.9), kind=kLoop, calls=%fused_computation | loop fusion | flops 65536 | bytes 524292 | tf_op jit(solution)/shard_map/mul | solution.py:518

commit v5 on v4

--- a/solution.py
+++ b/solution.py
@@ -467,7 +467,7 @@
     hbm = pl.BlockSpec(memory_space=pltpu.HBM)
     grads = pl.pallas_call(
         kernel,
-        out_shape=jax.ShapeDtypeStruct((2, own, ds), F32),
+        out_shape=pltpu.VMEM((2, own, ds), F32),
         in_specs=[smem, smem, hbm, hbm, hbm, hbm],
         out_specs=vmem,
         scratch_shapes=[

time: 59.2 us -> 57.6 us (0.973)
  other arithmetic: 1.69 us -> 0.72 us
  Pallas kernels: 55.5 us -> 54.8 us
    mul x1, other arithmetic: 1.69 us -> 0.72 us  [body(): return (grads[0] * student_scale, grads[1] * student_scale)]
    pallas_call x1, Pallas kernels: 55.5 us -> 54.8 us  [body(): pl.pallas_call(kernel, out_shape=pltpu.VMEM((2, own, ds), F32), in_specs=...]
where the time goes in v5:
time: 57.6 us; the launch traced here: 57.4 us
  Pallas kernels  54.8 us (95%)
  between operations  1.93 us (3%)
  other arithmetic  0.72 us (1%)
    pallas_call x1, Pallas kernels, body(): pl.pallas_call(kernel, out_shape=pltpu.VMEM((2, own, ds), F32), in_specs=...  54.8 us

profile of v5, /device:TPU:1, one launch (start us, length us, event | category | flops | bytes accessed | tf_op | source)
XLA Modules:
  0.0 57.4 jit_solution(6411960194449202713)
XLA Ops:
  1.9 54.8 %shard_map.77 = f32[2,64,512]{2,1,0:T(8,128)S(1)} custom-call(f32[1,1]{1,0:T(1,128)} %bitcast.6.tscale_ref, f32[1,1]{1,0:T(1,128)} %bitcast.7.sscale_ref, bf16[64,512]{1,0:T(8,128)(2,1)} %si_hbm.1, bf16[64,512]{1,0:T(8,128)(2,1)} %st_hbm.1, bf16[64,1280]{1,0:T(8,128)(2,1)} %ti_hbm.1, bf16[64,1280]{1,0:T(8,128)(2,1)} %tt_hbm.1), custom_call_target="tpu_custom_call" | custom-call | tf_op jit(solution)/shard_map/pallas_call | solution.py:468
  56.7 0.7 %multiply_bitcast_fusion = (f32[64,512]{1,0:T(8,128)}, f32[64,512]{1,0:T(8,128)}) fusion(f32[2,64,512]{2,1,0:T(8,128)S(1)} %shard_map.77, f32[]{:T(128)} %copy.9), kind=kLoop, calls=%fused_computation | loop fusion | flops 65536 | bytes 524292 | tf_op jit(solution)/shard_map/mul | solution.py:518

commit v6 on v5

--- a/solution.py
+++ b/solution.py
@@ -13,7 +13,7 @@
 NX, NY, NZ = 4, 4, 8
 LOG2E = math.log2(math.e)
 F32, BF16 = jnp.float32, jnp.bfloat16
-SEMAPHORES = 64
+SEMAPHORES = 57
 
 PAIRS = (
     ((0, 0), (1, 0)),
@@ -235,11 +235,10 @@
     text_arrive(2, 1)
     second_axis_arrive(1)
     text_arrive(2, 2)
-    logits(3, 4, 0)
     text_arrive(2, 3)
     second_axis_arrive(3)
     text_arrive(3, 0)
-    logits(4, 5, 0)
+    logits(3, 5, 0)
     sibling_arrive(2, 2)
     logits(0, 3, 1)
     text_arrive(3, 1)

time: 57.6 us -> 57.5 us (level)
  no operation moved by 1% of the time
where the time goes in v6:
time: 57.5 us; the launch traced here: 57.4 us
  Pallas kernels  54.7 us (95%)
  between operations  1.93 us (3%)
  other arithmetic  0.72 us (1%)
    pallas_call x1, Pallas kernels, body(): pl.pallas_call(kernel, out_shape=pltpu.VMEM((2, own, ds), F32), in_specs=...  54.7 us

profile of v6, /device:TPU:1, one launch (start us, length us, event | category | flops | bytes accessed | tf_op | source)
XLA Modules:
  0.0 57.4 jit_solution(10667985801615764825)
XLA Ops:
  1.9 54.7 %shard_map.77 = f32[2,64,512]{2,1,0:T(8,128)S(1)} custom-call(f32[1,1]{1,0:T(1,128)} %bitcast.6.tscale_ref, f32[1,1]{1,0:T(1,128)} %bitcast.7.sscale_ref, bf16[64,512]{1,0:T(8,128)(2,1)} %si_hbm.1, bf16[64,512]{1,0:T(8,128)(2,1)} %st_hbm.1, bf16[64,1280]{1,0:T(8,128)(2,1)} %ti_hbm.1, bf16[64,1280]{1,0:T(8,128)(2,1)} %tt_hbm.1), custom_call_target="tpu_custom_call" | custom-call | tf_op jit(solution)/shard_map/pallas_call | solution.py:467
  56.7 0.7 %multiply_bitcast_fusion = (f32[64,512]{1,0:T(8,128)}, f32[64,512]{1,0:T(8,128)}) fusion(f32[2,64,512]{2,1,0:T(8,128)S(1)} %shard_map.77, f32[]{:T(128)} %copy.9), kind=kLoop, calls=%fused_computation | loop fusion | flops 65536 | bytes 524292 | tf_op jit(solution)/shard_map/mul | solution.py:517
